TPU v7x, 32 devices: a whole 2x2x4 slice. The times are simulated.
32 devices in a mesh: grp: 4 (over x, core), seq: 8 (over z, y).
Axes of the slice: x: 2, y: 2, z: 4, core: 2. Of those that a mesh axis runs over, the one named last changes fastest.
Arguments:
- queries: bfloat16 [16384, 1024], P(('grp', 'seq')), may hold values from -8 to 8
- keys: bfloat16 [16384, 1024], P(('grp', 'seq')), may hold values from -8 to 8
- values: bfloat16 [16384, 1024], P(('grp', 'seq')), may hold values from -6 to 6
- event_ids: int32 [16384], P(('grp', 'seq')), may hold values from 0 to 511
- type_bias: float32 [512, 16], replicated, may hold values from -4 to 4
- block_start: int32 [32, 5], P(('grp', 'seq')), may hold values from 0 to 448
- d_out: bfloat16 [16384, 1024], P(('grp', 'seq')), may hold values from -6 to 6
Outputs:
- out: bfloat16 [16384, 1024], P(('grp', 'seq'))
- d_queries: bfloat16 [16384, 1024], P(('grp', 'seq'))
- d_keys: bfloat16 [16384, 1024], P(('grp', 'seq'))
- d_values: bfloat16 [16384, 1024], P(('grp', 'seq'))
All inputs are finite; a program needn't handle non-finite values.
Results may differ from a plain program's by a relative error of at most 0.011.
Values may be sent and summed in bfloat16 or wider, within the bound.
A program may use at most 128 MiB of HBM per device.

v0:
```python
import math

import jax
import jax.numpy as jnp
from jax import lax
from jax.sharding import PartitionSpec as P

WIN = 256
BLK = 64


def as_sent(shard):

    def short(part):
        return part.astype(jnp.bfloat16) if part.dtype == jnp.float32 else part

    return jax.tree.map(short, shard)


def passed_along(value, axis, steps):
    count = lax.axis_size(axis)
    initial, last = (max(0, -steps), min(count, count - steps))
    return lax.ppermute(value, axis, [(source, source + steps) for source in range(initial, last)])


def lookup_bias(event_ids, type_bias):
    type_count = type_bias.shape[0]
    onehot = (event_ids[:, None] == jnp.arange(type_count, dtype=jnp.int32)[None, :]).astype(
        jnp.float32
    )
    return jnp.dot(onehot, type_bias, precision=lax.Precision.HIGHEST).astype(jnp.bfloat16)


def send_forward(payload, distance):
    arrived = jax.tree.map(
        lambda part, own: part.astype(own.dtype),
        passed_along(as_sent(payload), ("grp", "seq"), distance),
        payload,
    )
    return arrived


def send_back(payload, distance):
    returned = passed_along((payload[0], payload[1]), ("grp", "seq"), -distance)
    return returned


def attend_group(
    query_cols,
    grad_cols,
    near_keys,
    near_values,
    near_bias,
    far_keys,
    far_values,
    far_bias,
    tail_live,
    far_live,
):
    row_count, column_width = query_cols.shape
    group_size = near_bias.shape[1]
    head_size = column_width // group_size
    window = near_keys.shape[0] - row_count
    far_count = far_keys.shape[0]
    score_scale = 1.0 / math.sqrt(head_size)
    block_rows = min(512, row_count)
    span_rows = block_rows + window
    far_key_heads = far_keys.reshape(far_count, group_size, head_size)
    far_value_heads = far_values.reshape(far_count, group_size, head_size)
    far_bias_rows = far_bias.astype(jnp.float32).T[:, None, :]
    near_key_grads = jnp.zeros((window + row_count, column_width), jnp.float32)
    near_value_grads = jnp.zeros((window + row_count, column_width), jnp.float32)
    query_heads = query_cols.reshape(block_rows, group_size, head_size)
    grad_heads = grad_cols.reshape(block_rows, group_size, head_size)
    key_heads = near_keys.reshape(span_rows, group_size, head_size)
    value_heads = near_values.reshape(span_rows, group_size, head_size)
    bias_rows = near_bias.astype(jnp.float32).T[:, None, :]
    row_index = jnp.arange(block_rows)[:, None]
    col_index = jnp.arange(span_rows)[None, :]
    near_mask = (col_index >= row_index) & (col_index <= row_index + window)
    near_mask = near_mask & ((col_index + 0 >= window) | tail_live)
    near_scores = (
        jnp.einsum("qhd,khd->hqk", query_heads, key_heads, preferred_element_type=jnp.float32)
        * score_scale
        + bias_rows
    )
    far_scores = (
        jnp.einsum("qhd,khd->hqk", query_heads, far_key_heads, preferred_element_type=jnp.float32)
        * score_scale
        + far_bias_rows
    )
    near_scores = jnp.where(near_mask[None], near_scores, -jnp.inf)
    far_scores = jnp.where(far_live[None, None, :], far_scores, -jnp.inf)
    highest = jnp.maximum(jnp.max(near_scores, axis=-1), jnp.max(far_scores, axis=-1))[:, :, None]
    near_exp = jnp.exp(near_scores - highest)
    far_exp = jnp.exp(far_scores - highest)
    normalizer = jnp.sum(near_exp, axis=-1, keepdims=True) + jnp.sum(
        far_exp, axis=-1, keepdims=True
    )
    near_weights = near_exp / normalizer
    far_weights = far_exp / normalizer
    near_rounded = near_weights.astype(jnp.bfloat16)
    far_rounded = far_weights.astype(jnp.bfloat16)
    attended = jnp.einsum(
        "hqk,khd->qhd", near_rounded, value_heads, preferred_element_type=jnp.float32
    )
    attended = attended + jnp.einsum(
        "hqk,khd->qhd", far_rounded, far_value_heads, preferred_element_type=jnp.float32
    )
    row_dot = jnp.sum(grad_heads.astype(jnp.float32) * attended, axis=-1).T[:, :, None]
    near_dw = jnp.einsum(
        "qhd,khd->hqk", grad_heads, value_heads, preferred_element_type=jnp.float32
    )
    far_dw = jnp.einsum(
        "qhd,khd->hqk", grad_heads, far_value_heads, preferred_element_type=jnp.float32
    )
    near_ds = (near_weights * (near_dw - row_dot)).astype(jnp.bfloat16)
    far_ds = (far_weights * (far_dw - row_dot)).astype(jnp.bfloat16)
    query_grad = jnp.einsum("hqk,khd->qhd", near_ds, key_heads, preferred_element_type=jnp.float32)
    query_grad = (
        query_grad
        + jnp.einsum("hqk,khd->qhd", far_ds, far_key_heads, preferred_element_type=jnp.float32)
    ) * score_scale
    near_key_part = (
        jnp.einsum("hqk,qhd->khd", near_ds, query_heads, preferred_element_type=jnp.float32)
        * score_scale
    )
    near_value_part = jnp.einsum(
        "hqk,qhd->khd", near_rounded, grad_heads, preferred_element_type=jnp.float32
    )
    far_key_part = (
        jnp.einsum("hqk,qhd->khd", far_ds, query_heads, preferred_element_type=jnp.float32)
        * score_scale
    )
    far_value_part = jnp.einsum(
        "hqk,qhd->khd", far_rounded, grad_heads, preferred_element_type=jnp.float32
    )
    near_key_grads = near_key_grads.at[0:span_rows].add(
        near_key_part.reshape(span_rows, column_width)
    )
    near_value_grads = near_value_grads.at[0:span_rows].add(
        near_value_part.reshape(span_rows, column_width)
    )
    far_key_grads = far_key_part.reshape(far_count, column_width)
    far_value_grads = far_value_part.reshape(far_count, column_width)
    attended_parts = [attended.reshape(block_rows, column_width)]
    query_parts = [query_grad.reshape(block_rows, column_width)]
    return (
        jnp.concatenate(attended_parts, axis=0),
        jnp.concatenate(query_parts, axis=0),
        near_key_grads,
        near_value_grads,
        far_key_grads,
        far_value_grads,
    )


def add_block(totals, arrived, offset):
    current = lax.dynamic_slice_in_dim(totals, offset, BLK, 0)
    return lax.dynamic_update_slice_in_dim(totals, current + arrived.astype(jnp.float32), offset, 0)


def local(queries, keys, values, event_ids, type_bias, block_start, d_out):
    row_count, width_all = queries.shape
    head_count = type_bias.shape[1]
    head_size = width_all // head_count
    level_count = block_start.shape[1]
    key_bias = lookup_bias(event_ids, type_bias)
    position = lax.axis_index(("grp", "seq"))
    tail_keys, tail_values, tail_bias = passed_along(
        (keys[row_count - WIN :], values[row_count - WIN :], key_bias[row_count - WIN :]),
        ("grp", "seq"),
        1,
    )
    far_parts = []
    for degree in range(level_count):
        offset = block_start[0, degree]
        payload = tuple(
            (
                lax.dynamic_slice_in_dim(source, offset, BLK, 0)
                for source in (keys, values, key_bias)
            )
        )
        far_parts.append(send_forward(payload, 2**degree))
    far_keys = jnp.concatenate([arrived[0] for arrived in far_parts], axis=0)
    far_values = jnp.concatenate([arrived[1] for arrived in far_parts], axis=0)
    far_bias = jnp.concatenate([arrived[2] for arrived in far_parts], axis=0)
    level_flags = position >= 2 ** jnp.arange(level_count, dtype=jnp.int32)
    far_live = jnp.repeat(level_flags, BLK, total_repeat_length=level_count * BLK)
    tail_live = position >= 1
    near_keys = jnp.concatenate([tail_keys, keys], axis=0)
    near_values = jnp.concatenate([tail_values, values], axis=0)
    near_bias = jnp.concatenate([tail_bias, key_bias], axis=0)
    group_size = min(4, head_count)
    column_width = group_size * head_size
    far_count = level_count * BLK
    start_state = (
        jnp.zeros((row_count, width_all), jnp.float32),
        jnp.zeros((row_count, width_all), jnp.float32),
        jnp.zeros((WIN + row_count, width_all), jnp.float32),
        jnp.zeros((WIN + row_count, width_all), jnp.float32),
        jnp.zeros((far_count, width_all), jnp.float32),
        jnp.zeros((far_count, width_all), jnp.float32),
    )

    def one_group(group_turn, carried):
        column = group_turn * column_width
        bias_column = group_turn * group_size

        def columns_of(array):
            return lax.dynamic_slice_in_dim(array, column, column_width, 1)

        def heads_of(array):
            return lax.dynamic_slice_in_dim(array, bias_column, group_size, 1)

        results = attend_group(
            columns_of(queries),
            columns_of(d_out),
            columns_of(near_keys),
            columns_of(near_values),
            heads_of(near_bias),
            columns_of(far_keys),
            columns_of(far_values),
            heads_of(far_bias),
            tail_live,
            far_live,
        )
        return tuple(
            (
                lax.dynamic_update_slice_in_dim(full_array, new_part, column, 1)
                for full_array, new_part in zip(carried, results)
            )
        )

    attended, query_grads, near_key_grads, near_value_grads, far_key_grads, far_value_grads = (
        lax.fori_loop(0, head_count // group_size, one_group, start_state)
    )
    returned_tail = passed_along(
        (near_key_grads[:WIN].astype(jnp.bfloat16), near_value_grads[:WIN].astype(jnp.bfloat16)),
        ("grp", "seq"),
        -1,
    )
    key_total = near_key_grads[WIN:].at[row_count - WIN :].add(returned_tail[0].astype(jnp.float32))
    value_total = (
        near_value_grads[WIN:].at[row_count - WIN :].add(returned_tail[1].astype(jnp.float32))
    )
    for degree in range(level_count):
        offset = block_start[0, degree]
        payload = (
            far_key_grads[degree * BLK : (degree + 1) * BLK].astype(jnp.bfloat16),
            far_value_grads[degree * BLK : (degree + 1) * BLK].astype(jnp.bfloat16),
        )
        returned = send_back(payload, 2**degree)
        key_total = add_block(key_total, returned[0], offset)
        value_total = add_block(value_total, returned[1], offset)
    return (
        attended.astype(jnp.bfloat16),
        query_grads.astype(jnp.bfloat16),
        key_total.astype(jnp.bfloat16),
        value_total.astype(jnp.bfloat16),
    )


def solution(mesh):
    return jax.shard_map(
        local,
        mesh=mesh,
        in_specs=(
            P(("grp", "seq"), None),
            P(("grp", "seq"), None),
            P(("grp", "seq"), None),
            P(("grp", "seq")),
            P(),
            P(("grp", "seq"), None),
            P(("grp", "seq"), None),
        ),
        out_specs=(
            P(("grp", "seq"), None),
            P(("grp", "seq"), None),
            P(("grp", "seq"), None),
            P(("grp", "seq"), None),
        ),
        check_vma=False,
    )
```

profile of v0, /device:TPU:2, one launch (start us, length us, event | category | flops | bytes accessed | tf_op | source)
XLA Modules:
  0.0 365.3 jit_solution(2551623194424365002)
XLA Ops:
  13.4 4.5 %collective-permute-start.10 = (bf16[64,16]{0,1:T(8,128)(2,1)S(1)}, bf16[64,16]{0,1:T(8,128)(2,1)S(1)}, u32[]{:S(2)}, u32[]{:S(2)}) collective-permute-start(bf16[64,16]{0,1:T(8,128)(2,1)S(1)} %get-tuple-element.474), channel_id=1, source_target_pairs={{0,4},{1,5},{2,6},{3,7},{4,8},{5,9},{6,10},{7,11},{8,12},{9,13},{1... | collective-permute-start | bytes 6152 | tf_op jit(solution)/shard_map/ppermute | solution.py:23
  21.1 3.4 collective-permute-start.8
  24.5 3.5 collective-permute-start.9
  36.8 4.0 %collective-permute-start.5 = (bf16[64,1024]{0,1:T(8,128)(2,1)}, bf16[64,1024]{0,1:T(8,128)(2,1)}, u32[]{:S(2)}, u32[]{:S(2)}) collective-permute-start(bf16[64,1024]{0,1:T(8,128)(2,1)} %get-tuple-element.459), channel_id=1, source_target_pairs={{0,4},{1,5},{2,6},{3,7},{4,8},{5,9},{6,10},{7,11},{8,12},{9,13},{1... | collective-permute-start | bytes 393224 | tf_op jit(solution)/shard_map/ppermute | solution.py:23
  42.7 3.1 collective-permute-start.2
  47.4 10.6 %collective-permute-done.2 = bf16[256,16]{0,1:T(8,128)(2,1)S(1)} collective-permute-done((bf16[256,16]{0,1:T(8,128)(2,1)S(1)}, bf16[256,16]{0,1:T(8,128)(2,1)S(1)}, u32[]{:S(2)}, u32[]{:S(2)}) %collective-permute-start.2) | collective-permute-done | bytes 8224 | tf_op jit(solution)/shard_map/ppermute | solution.py:23
  63.2 4.6 %collective-permute-start = (bf16[256,1024]{0,1:T(8,128)(2,1)S(1)}, bf16[256,1024]{0,1:T(8,128)(2,1)}, u32[]{:S(2)}, u32[]{:S(2)}) collective-permute-start(bf16[256,1024]{0,1:T(8,128)(2,1)S(1)} %slice.203), channel_id=1, source_target_pairs={{0,1},{1,2},{2,3},{3,4},{4,5},{5,6},{6,7},{7,8},{8,9},{9,10},{10,1... | collective-permute-start | bytes 1572872 | tf_op jit(solution)/shard_map/ppermute | solution.py:23
  78.4 3.1 select_select_fusion
  84.0 4.2 %collective-permute-done.15 = bf16[64,1024]{0,1:T(8,128)(2,1)} collective-permute-done((bf16[64,1024]{0,1:T(8,128)(2,1)}, bf16[64,1024]{0,1:T(8,128)(2,1)}, u32[]{:S(2)}, u32[]{:S(2)}) %collective-permute-start.15) | collective-permute-done | bytes 131104 | tf_op jit(solution)/shard_map/ppermute | solution.py:23
  88.2 2.9 collective-permute-done.17
  95.7 6.1 %collective-permute-done.1 = bf16[256,1024]{0,1:T(8,128)(2,1)} collective-permute-done((bf16[256,1024]{0,1:T(8,128)(2,1)S(1)}, bf16[256,1024]{0,1:T(8,128)(2,1)}, u32[]{:S(2)}, u32[]{:S(2)}) %collective-permute-start.1) | collective-permute-done | bytes 524320 | tf_op jit(solution)/shard_map/ppermute | solution.py:23
  111.3 167.2 %while.38 = (s32[]{:T(128)}, bf16[512,1024]{1,0:T(8,128)(2,1)}, bf16[512,1024]{1,0:T(8,128)(2,1)}, f32[768,1024]{1,0:T(8,128)}, f32[768,1024]{1,0:T(8,128)}, /*i...) while((s32[]{:T(128)}, bf16[512,1024]{1,0:T(8,128)(2,1)}, ...), condition=%wide.region_6.7_spmd, body=%wide.region_0.6_spmd.sunk | while | flops 1769046272 | bytes 163947632 | solution.py:236
  123.5 6.0 %fusion.122 = (f32[512,4]{0,1:T(4,128)S(1)}, bf16[4,64,512]{2,1,0:T(8,128)(2,1)}) fusion(bf16[512,256]{0,1:T(8,128)(2,1)S(1)} %copy.59, f32[4,64,512]{2,1,0:T(8,128)S(1)} %fusion.121, bf16[768,4,64]{0,2,1:T(8,128)(2,1)S(1)} %bitcast.165, f32[4,512]{1,0:T(4,128)S(1)} %add.357, f32[4,512]{1,0:T(4,128)S(1)} %max.12, ...), kind=kOutput, calls=%fused_computation.26.clone.1 | convolution fusion | flops 211417088 | bytes 8163328 | tf_op jit(solution)/shard_map/while/body/eval_jaxpr/hqk,khd->qhd/dot_general | solution.py:104
  133.4 4.4 %fusion.125 = f32[4,64,768]{2,1,0:T(8,128)S(1)} fusion(bf16[512,4,64]{0,2,1:T(8,128)(2,1)S(1)} %bitcast.155, f32[4,512,768]{2,1,0:T(8,128)} %copy-done.3, f32[4,512]{1,0:T(4,128)S(1)} %add.357, f32[4,512]{1,0:T(4,128)S(1)} %max.12, f32[4,768]{1,0:T(4,128)S(1)} %convert_bitcast_fusion.4, pred[512,768]{1,0:T(8,128)(4,1)S(1)} %fusion.115), kind=kOutput, calls=%fused_computation.11.clone.1 | convolution fusion | flops 210763776 | bytes 7761920 | tf_op jit(solution)/shard_map/while/body/eval_jaxpr/hqk,qhd->khd/dot_general | solution.py:128
  138.9 4.9 %multiply_convert_fusion.4 = bf16[4,512,768]{2,1,0:T(8,128)(2,1)S(1)} fusion(f32[4,512]{1,0:T(4,128)S(1)} %bitcast.169, bf16[512,4,64]{0,2,1:T(8,128)(2,1)} %bitcast.156, bf16[768,4,64]{0,2,1:T(8,128)(2,1)} %bitcast.166, f32[4,512]{1,0:T(4,128)S(1)} %add.357, f32[4,512]{1,0:T(4,128)S(1)} %max.12, f32[4,768]{1,0:T(4,128)S(1)} %convert_bitcast_fusion.4, ...), kind=kOutput, calls=%fused_computation.clone.1 | convolution fusion | flops 213909504 | bytes 10522624 | tf_op jit(solution)/shard_map/while/body/eval_jaxpr/qhd,khd->hqk/dot_general | solution.py:111
  147.7 2.8 constant_dynamic-update-slice_fusion.10
  165.3 6.0 %fusion.122 = (f32[512,4]{0,1:T(4,128)S(1)}, bf16[4,64,512]{2,1,0:T(8,128)(2,1)}) fusion(bf16[512,256]{0,1:T(8,128)(2,1)S(1)} %copy.59, f32[4,64,512]{2,1,0:T(8,128)S(1)} %fusion.121, bf16[768,4,64]{0,2,1:T(8,128)(2,1)S(1)} %bitcast.165, f32[4,512]{1,0:T(4,128)S(1)} %add.357, f32[4,512]{1,0:T(4,128)S(1)} %max.12, ...), kind=kOutput, calls=%fused_computation.26.clone.1 | convolution fusion | flops 211417088 | bytes 8163328 | tf_op jit(solution)/shard_map/while/body/eval_jaxpr/hqk,khd->qhd/dot_general | solution.py:104
  175.2 4.4 %fusion.125 = f32[4,64,768]{2,1,0:T(8,128)S(1)} fusion(bf16[512,4,64]{0,2,1:T(8,128)(2,1)S(1)} %bitcast.155, f32[4,512,768]{2,1,0:T(8,128)} %copy-done.3, f32[4,512]{1,0:T(4,128)S(1)} %add.357, f32[4,512]{1,0:T(4,128)S(1)} %max.12, f32[4,768]{1,0:T(4,128)S(1)} %convert_bitcast_fusion.4, pred[512,768]{1,0:T(8,128)(4,1)S(1)} %fusion.115), kind=kOutput, calls=%fused_computation.11.clone.1 | convolution fusion | flops 210763776 | bytes 7761920 | tf_op jit(solution)/shard_map/while/body/eval_jaxpr/hqk,qhd->khd/dot_general | solution.py:128
  180.7 4.9 %multiply_convert_fusion.4 = bf16[4,512,768]{2,1,0:T(8,128)(2,1)S(1)} fusion(f32[4,512]{1,0:T(4,128)S(1)} %bitcast.169, bf16[512,4,64]{0,2,1:T(8,128)(2,1)} %bitcast.156, bf16[768,4,64]{0,2,1:T(8,128)(2,1)} %bitcast.166, f32[4,512]{1,0:T(4,128)S(1)} %add.357, f32[4,512]{1,0:T(4,128)S(1)} %max.12, f32[4,768]{1,0:T(4,128)S(1)} %convert_bitcast_fusion.4, ...), kind=kOutput, calls=%fused_computation.clone.1 | convolution fusion | flops 213909504 | bytes 10522624 | tf_op jit(solution)/shard_map/while/body/eval_jaxpr/qhd,khd->hqk/dot_general | solution.py:111
  207.1 6.0 %fusion.122 = (f32[512,4]{0,1:T(4,128)S(1)}, bf16[4,64,512]{2,1,0:T(8,128)(2,1)}) fusion(bf16[512,256]{0,1:T(8,128)(2,1)S(1)} %copy.59, f32[4,64,512]{2,1,0:T(8,128)S(1)} %fusion.121, bf16[768,4,64]{0,2,1:T(8,128)(2,1)S(1)} %bitcast.165, f32[4,512]{1,0:T(4,128)S(1)} %add.357, f32[4,512]{1,0:T(4,128)S(1)} %max.12, ...), kind=kOutput, calls=%fused_computation.26.clone.1 | convolution fusion | flops 211417088 | bytes 8163328 | tf_op jit(solution)/shard_map/while/body/eval_jaxpr/hqk,khd->qhd/dot_general | solution.py:104
  217.0 4.4 %fusion.125 = f32[4,64,768]{2,1,0:T(8,128)S(1)} fusion(bf16[512,4,64]{0,2,1:T(8,128)(2,1)S(1)} %bitcast.155, f32[4,512,768]{2,1,0:T(8,128)} %copy-done.3, f32[4,512]{1,0:T(4,128)S(1)} %add.357, f32[4,512]{1,0:T(4,128)S(1)} %max.12, f32[4,768]{1,0:T(4,128)S(1)} %convert_bitcast_fusion.4, pred[512,768]{1,0:T(8,128)(4,1)S(1)} %fusion.115), kind=kOutput, calls=%fused_computation.11.clone.1 | convolution fusion | flops 210763776 | bytes 7761920 | tf_op jit(solution)/shard_map/while/body/eval_jaxpr/hqk,qhd->khd/dot_general | solution.py:128
  222.5 4.9 %multiply_convert_fusion.4 = bf16[4,512,768]{2,1,0:T(8,128)(2,1)S(1)} fusion(f32[4,512]{1,0:T(4,128)S(1)} %bitcast.169, bf16[512,4,64]{0,2,1:T(8,128)(2,1)} %bitcast.156, bf16[768,4,64]{0,2,1:T(8,128)(2,1)} %bitcast.166, f32[4,512]{1,0:T(4,128)S(1)} %add.357, f32[4,512]{1,0:T(4,128)S(1)} %max.12, f32[4,768]{1,0:T(4,128)S(1)} %convert_bitcast_fusion.4, ...), kind=kOutput, calls=%fused_computation.clone.1 | convolution fusion | flops 213909504 | bytes 10522624 | tf_op jit(solution)/shard_map/while/body/eval_jaxpr/qhd,khd->hqk/dot_general | solution.py:111
  248.9 6.0 %fusion.122 = (f32[512,4]{0,1:T(4,128)S(1)}, bf16[4,64,512]{2,1,0:T(8,128)(2,1)}) fusion(bf16[512,256]{0,1:T(8,128)(2,1)S(1)} %copy.59, f32[4,64,512]{2,1,0:T(8,128)S(1)} %fusion.121, bf16[768,4,64]{0,2,1:T(8,128)(2,1)S(1)} %bitcast.165, f32[4,512]{1,0:T(4,128)S(1)} %add.357, f32[4,512]{1,0:T(4,128)S(1)} %max.12, ...), kind=kOutput, calls=%fused_computation.26.clone.1 | convolution fusion | flops 211417088 | bytes 8163328 | tf_op jit(solution)/shard_map/while/body/eval_jaxpr/hqk,khd->qhd/dot_general | solution.py:104
  258.8 4.4 %fusion.125 = f32[4,64,768]{2,1,0:T(8,128)S(1)} fusion(bf16[512,4,64]{0,2,1:T(8,128)(2,1)S(1)} %bitcast.155, f32[4,512,768]{2,1,0:T(8,128)} %copy-done.3, f32[4,512]{1,0:T(4,128)S(1)} %add.357, f32[4,512]{1,0:T(4,128)S(1)} %max.12, f32[4,768]{1,0:T(4,128)S(1)} %convert_bitcast_fusion.4, pred[512,768]{1,0:T(8,128)(4,1)S(1)} %fusion.115), kind=kOutput, calls=%fused_computation.11.clone.1 | convolution fusion | flops 210763776 | bytes 7761920 | tf_op jit(solution)/shard_map/while/body/eval_jaxpr/hqk,qhd->khd/dot_general | solution.py:128
  264.3 4.9 %multiply_convert_fusion.4 = bf16[4,512,768]{2,1,0:T(8,128)(2,1)S(1)} fusion(f32[4,512]{1,0:T(4,128)S(1)} %bitcast.169, bf16[512,4,64]{0,2,1:T(8,128)(2,1)} %bitcast.156, bf16[768,4,64]{0,2,1:T(8,128)(2,1)} %bitcast.166, f32[4,512]{1,0:T(4,128)S(1)} %add.357, f32[4,512]{1,0:T(4,128)S(1)} %max.12, f32[4,768]{1,0:T(4,128)S(1)} %convert_bitcast_fusion.4, ...), kind=kOutput, calls=%fused_computation.clone.1 | convolution fusion | flops 213909504 | bytes 10522624 | tf_op jit(solution)/shard_map/while/body/eval_jaxpr/qhd,khd->hqk/dot_general | solution.py:111
  273.0 2.8 constant_dynamic-update-slice_fusion.10
  279.9 15.4 %collective-permute-start.24 = (bf16[256,1024]{1,0:T(8,128)(2,1)S(1)}, bf16[256,1024]{1,0:T(8,128)(2,1)S(1)}, u32[]{:S(2)}, u32[]{:S(2)}) collective-permute-start(bf16[256,1024]{1,0:T(8,128)(2,1)S(1)} %slice.225), channel_id=1, source_target_pairs={{1,0},{2,1},{3,2},{4,3},{5,4},{6,5},{7,6},{8,7},{9,8},{10,9},{11,1... | collective-permute-start | bytes 1572872 | tf_op jit(solution)/shard_map/ppermute | solution.py:23
  300.8 4.0 %collective-permute-start.26 = (bf16[64,1024]{1,0:T(8,128)(2,1)}, bf16[64,1024]{1,0:T(8,128)(2,1)}, u32[]{:S(2)}, u32[]{:S(2)}) collective-permute-start(bf16[64,1024]{1,0:T(8,128)(2,1)} %get-tuple-element.465), channel_id=1, source_target_pairs={{2,0},{3,1},{4,2},{5,3},{6,4},{7,5},{8,6},{9,7},{10,8},{11,9},{12,... | collective-permute-start | bytes 393224 | tf_op jit(solution)/shard_map/ppermute | solution.py:23
  304.8 3.8 %collective-permute-start.27 = (bf16[64,1024]{1,0:T(8,128)(2,1)S(1)}, bf16[64,1024]{1,0:T(8,128)(2,1)}, u32[]{:S(2)}, u32[]{:S(2)}) collective-permute-start(bf16[64,1024]{1,0:T(8,128)(2,1)S(1)} %get-tuple-element.464), channel_id=1, source_target_pairs={{4,0},{5,1},{6,2},{7,3},{8,4},{9,5},{10,6},{11,7},{12,8},{13,9},{1... | collective-permute-start | bytes 393224 | tf_op jit(solution)/shard_map/ppermute | solution.py:23
  308.7 5.2 %collective-permute-start.18 = (bf16[256,1024]{1,0:T(8,128)(2,1)S(1)}, bf16[256,1024]{1,0:T(8,128)(2,1)S(1)}, u32[]{:S(2)}, u32[]{:S(2)}) collective-permute-start(bf16[256,1024]{1,0:T(8,128)(2,1)S(1)} %slice.226), channel_id=1, source_target_pairs={{1,0},{2,1},{3,2},{4,3},{5,4},{6,5},{7,6},{8,7},{9,8},{10,9},{11,1... | collective-permute-start | bytes 1572872 | tf_op jit(solution)/shard_map/ppermute | solution.py:23
  317.2 8.8 %collective-permute-done.18 = bf16[256,1024]{1,0:T(8,128)(2,1)S(1)} collective-permute-done((bf16[256,1024]{1,0:T(8,128)(2,1)S(1)}, bf16[256,1024]{1,0:T(8,128)(2,1)S(1)}, u32[]{:S(2)}, u32[]{:S(2)}) %collective-permute-start.18) | collective-permute-done | bytes 524320 | tf_op jit(solution)/shard_map/ppermute | solution.py:23
  326.0 7.7 %collective-permute-start.19 = (bf16[64,1024]{1,0:T(8,128)(2,1)S(1)}, bf16[64,1024]{1,0:T(8,128)(2,1)}, u32[]{:S(2)}, u32[]{:S(2)}) collective-permute-start(bf16[64,1024]{1,0:T(8,128)(2,1)S(1)} %get-tuple-element.471), channel_id=1, source_target_pairs={{1,0},{2,1},{3,2},{4,3},{5,4},{6,5},{7,6},{8,7},{9,8},{10,9},{11,1... | collective-permute-start | bytes 393224 | tf_op jit(solution)/shard_map/ppermute | solution.py:23
  (383 shorter events, 191.2 us)
Async XLA Ops:
  0.6 31.2 %copy-start.20 = (bf16[512,1024]{1,0:T(8,128)(2,1)S(1)}, bf16[512,1024]{1,0:T(8,128)(2,1)}, u32[]{:S(2)}) copy-start(bf16[512,1024]{1,0:T(8,128)(2,1)} %param.25) | copy-start | bytes 3145732
  13.4 19.0 %collective-permute-start.10 = (bf16[64,16]{0,1:T(8,128)(2,1)S(1)}, bf16[64,16]{0,1:T(8,128)(2,1)S(1)}, u32[]{:S(2)}, u32[]{:S(2)}) collective-permute-start(bf16[64,16]{0,1:T(8,128)(2,1)S(1)} %get-tuple-element.474), channel_id=1, source_target_pairs={{0,4},{1,5},{2,6},{3,7},{4,8},{5,9},{6,10},{7,11},{8,12},{9,13},{1... | collective-permute-start | bytes 6152 | tf_op jit(solution)/shard_map/ppermute | solution.py:23
  17.9 16.4 %collective-permute-start.11 = (bf16[64,16]{0,1:T(8,128)(2,1)S(1)}, bf16[64,16]{0,1:T(8,128)(2,1)S(1)}, u32[]{:S(2)}, u32[]{:S(2)}) collective-permute-start(bf16[64,16]{0,1:T(8,128)(2,1)S(1)} %get-tuple-element.473), channel_id=1, source_target_pairs={{0,8},{1,9},{2,10},{3,11},{4,12},{5,13},{6,14},{7,15},{8,16},{9,17... | collective-permute-start | bytes 6152 | tf_op jit(solution)/shard_map/ppermute | solution.py:23
  19.8 17.0 %collective-permute-start.12 = (bf16[64,16]{0,1:T(8,128)(2,1)S(1)}, bf16[64,16]{0,1:T(8,128)(2,1)S(1)}, u32[]{:S(2)}, u32[]{:S(2)}) collective-permute-start(bf16[64,16]{0,1:T(8,128)(2,1)S(1)} %get-tuple-element.472), channel_id=1, source_target_pairs={{0,16},{1,17},{2,18},{3,19},{4,20},{5,21},{6,22},{7,23},{8,24},{9,... | collective-permute-start | bytes 6152 | tf_op jit(solution)/shard_map/ppermute | solution.py:23
  21.1 19.6 %collective-permute-start.8 = (bf16[64,16]{0,1:T(8,128)(2,1)S(1)}, bf16[64,16]{0,1:T(8,128)(2,1)S(1)}, u32[]{:S(2)}, u32[]{:S(2)}) collective-permute-start(bf16[64,16]{0,1:T(8,128)(2,1)S(1)} %get-tuple-element.476), channel_id=1, source_target_pairs={{0,1},{1,2},{2,3},{3,4},{4,5},{5,6},{6,7},{7,8},{8,9},{9,10},{10,1... | collective-permute-start | bytes 6152 | tf_op jit(solution)/shard_map/ppermute | solution.py:23
  24.5 18.2 %collective-permute-start.9 = (bf16[64,16]{0,1:T(8,128)(2,1)S(1)}, bf16[64,16]{0,1:T(8,128)(2,1)S(1)}, u32[]{:S(2)}, u32[]{:S(2)}) collective-permute-start(bf16[64,16]{0,1:T(8,128)(2,1)S(1)} %get-tuple-element.475), channel_id=1, source_target_pairs={{0,2},{1,3},{2,4},{3,5},{4,6},{5,7},{6,8},{7,9},{8,10},{9,11},{10,... | collective-permute-start | bytes 6152 | tf_op jit(solution)/shard_map/ppermute | solution.py:23
  32.4 26.9 %collective-permute-start.3 = (bf16[64,1024]{0,1:T(8,128)(2,1)}, bf16[64,1024]{0,1:T(8,128)(2,1)S(1)}, u32[]{:S(2)}, u32[]{:S(2)}) collective-permute-start(bf16[64,1024]{0,1:T(8,128)(2,1)} %get-tuple-element.461), channel_id=1, source_target_pairs={{0,1},{1,2},{2,3},{3,4},{4,5},{5,6},{6,7},{7,8},{8,9},{9,10},{10,1... | collective-permute-start | bytes 393224 | tf_op jit(solution)/shard_map/ppermute | solution.py:23
  34.3 26.9 %collective-permute-start.4 = (bf16[64,1024]{0,1:T(8,128)(2,1)}, bf16[64,1024]{0,1:T(8,128)(2,1)S(1)}, u32[]{:S(2)}, u32[]{:S(2)}) collective-permute-start(bf16[64,1024]{0,1:T(8,128)(2,1)} %get-tuple-element.460), channel_id=1, source_target_pairs={{0,2},{1,3},{2,4},{3,5},{4,6},{5,7},{6,8},{7,9},{8,10},{9,11},{10,... | collective-permute-start | bytes 393224 | tf_op jit(solution)/shard_map/ppermute | solution.py:23
  36.8 26.4 %collective-permute-start.5 = (bf16[64,1024]{0,1:T(8,128)(2,1)}, bf16[64,1024]{0,1:T(8,128)(2,1)}, u32[]{:S(2)}, u32[]{:S(2)}) collective-permute-start(bf16[64,1024]{0,1:T(8,128)(2,1)} %get-tuple-element.459), channel_id=1, source_target_pairs={{0,4},{1,5},{2,6},{3,7},{4,8},{5,9},{6,10},{7,11},{8,12},{9,13},{1... | collective-permute-start | bytes 393224 | tf_op jit(solution)/shard_map/ppermute | solution.py:23
  40.8 27.2 %collective-permute-start.6 = (bf16[64,1024]{0,1:T(8,128)(2,1)}, bf16[64,1024]{0,1:T(8,128)(2,1)}, u32[]{:S(2)}, u32[]{:S(2)}) collective-permute-start(bf16[64,1024]{0,1:T(8,128)(2,1)} %get-tuple-element.458), channel_id=1, source_target_pairs={{0,8},{1,9},{2,10},{3,11},{4,12},{5,13},{6,14},{7,15},{8,16},{9,17... | collective-permute-start | bytes 393224 | tf_op jit(solution)/shard_map/ppermute | solution.py:23
  42.7 15.3 %collective-permute-start.2 = (bf16[256,16]{0,1:T(8,128)(2,1)S(1)}, bf16[256,16]{0,1:T(8,128)(2,1)S(1)}, u32[]{:S(2)}, u32[]{:S(2)}) collective-permute-start(bf16[256,16]{0,1:T(8,128)(2,1)S(1)} %slice.205), channel_id=1, source_target_pairs={{0,1},{1,2},{2,3},{3,4},{4,5},{5,6},{6,7},{7,8},{8,9},{9,10},{10,1... | collective-permute-start | bytes 24584 | tf_op jit(solution)/shard_map/ppermute | solution.py:23
  58.0 12.6 %collective-permute-start.7 = (bf16[64,1024]{0,1:T(8,128)(2,1)}, bf16[64,1024]{0,1:T(8,128)(2,1)S(1)}, u32[]{:S(2)}, u32[]{:S(2)}) collective-permute-start(bf16[64,1024]{0,1:T(8,128)(2,1)} %get-tuple-element.457), channel_id=1, source_target_pairs={{0,16},{1,17},{2,18},{3,19},{4,20},{5,21},{6,22},{7,23},{8,24},{9,... | collective-permute-start | bytes 393224 | tf_op jit(solution)/shard_map/ppermute | solution.py:23
  59.3 15.8 %collective-permute-start.13 = (bf16[64,1024]{0,1:T(8,128)(2,1)}, bf16[64,1024]{0,1:T(8,128)(2,1)S(1)}, u32[]{:S(2)}, u32[]{:S(2)}) collective-permute-start(bf16[64,1024]{0,1:T(8,128)(2,1)} %get-tuple-element.456), channel_id=1, source_target_pairs={{0,1},{1,2},{2,3},{3,4},{4,5},{5,6},{6,7},{7,8},{8,9},{9,10},{10,1... | collective-permute-start | bytes 393224 | tf_op jit(solution)/shard_map/ppermute | solution.py:23
  61.2 15.8 %collective-permute-start.14 = (bf16[64,1024]{0,1:T(8,128)(2,1)}, bf16[64,1024]{0,1:T(8,128)(2,1)S(1)}, u32[]{:S(2)}, u32[]{:S(2)}) collective-permute-start(bf16[64,1024]{0,1:T(8,128)(2,1)} %get-tuple-element.455), channel_id=1, source_target_pairs={{0,2},{1,3},{2,4},{3,5},{4,6},{5,7},{6,8},{7,9},{8,10},{9,11},{10,... | collective-permute-start | bytes 393224 | tf_op jit(solution)/shard_map/ppermute | solution.py:23
  63.2 30.2 %collective-permute-start = (bf16[256,1024]{0,1:T(8,128)(2,1)S(1)}, bf16[256,1024]{0,1:T(8,128)(2,1)}, u32[]{:S(2)}, u32[]{:S(2)}) collective-permute-start(bf16[256,1024]{0,1:T(8,128)(2,1)S(1)} %slice.203), channel_id=1, source_target_pairs={{0,1},{1,2},{2,3},{3,4},{4,5},{5,6},{6,7},{7,8},{8,9},{9,10},{10,1... | collective-permute-start | bytes 1572872 | tf_op jit(solution)/shard_map/ppermute | solution.py:23
  67.9 33.9 %collective-permute-start.1 = (bf16[256,1024]{0,1:T(8,128)(2,1)S(1)}, bf16[256,1024]{0,1:T(8,128)(2,1)}, u32[]{:S(2)}, u32[]{:S(2)}) collective-permute-start(bf16[256,1024]{0,1:T(8,128)(2,1)S(1)} %slice.204), channel_id=1, source_target_pairs={{0,1},{1,2},{2,3},{3,4},{4,5},{5,6},{6,7},{7,8},{8,9},{9,10},{10,1... | collective-permute-start | bytes 1572872 | tf_op jit(solution)/shard_map/ppermute | solution.py:23
  70.5 17.7 %collective-permute-start.15 = (bf16[64,1024]{0,1:T(8,128)(2,1)}, bf16[64,1024]{0,1:T(8,128)(2,1)}, u32[]{:S(2)}, u32[]{:S(2)}) collective-permute-start(bf16[64,1024]{0,1:T(8,128)(2,1)} %get-tuple-element.454), channel_id=1, source_target_pairs={{0,4},{1,5},{2,6},{3,7},{4,8},{5,9},{6,10},{7,11},{8,12},{9,13},{1... | collective-permute-start | bytes 393224 | tf_op jit(solution)/shard_map/ppermute | solution.py:23
  75.1 13.1 %collective-permute-start.16 = (bf16[64,1024]{0,1:T(8,128)(2,1)}, bf16[64,1024]{0,1:T(8,128)(2,1)}, u32[]{:S(2)}, u32[]{:S(2)}) collective-permute-start(bf16[64,1024]{0,1:T(8,128)(2,1)} %get-tuple-element.453), channel_id=1, source_target_pairs={{0,8},{1,9},{2,10},{3,11},{4,12},{5,13},{6,14},{7,15},{8,16},{9,17... | collective-permute-start | bytes 393224 | tf_op jit(solution)/shard_map/ppermute | solution.py:23
  77.1 14.0 %collective-permute-start.17 = (bf16[64,1024]{0,1:T(8,128)(2,1)S(1)}, bf16[64,1024]{0,1:T(8,128)(2,1)}, u32[]{:S(2)}, u32[]{:S(2)}) collective-permute-start(bf16[64,1024]{0,1:T(8,128)(2,1)S(1)} %get-tuple-element.452), channel_id=1, source_target_pairs={{0,16},{1,17},{2,18},{3,19},{4,20},{5,21},{6,22},{7,23},{8,24},{9,... | collective-permute-start | bytes 393224 | tf_op jit(solution)/shard_map/ppermute | solution.py:23
  238.4 20.4 %copy-start.6 = (pred[512,768]{1,0:T(8,128)(4,1)}, pred[512,768]{1,0:T(8,128)(4,1)S(1)}, u32[]{:S(2)}) copy-start(pred[512,768]{1,0:T(8,128)(4,1)S(1)} %fusion.115) | copy-start | bytes 1179652 | tf_op jit(solution)/shard_map/while
  279.9 34.0 %collective-permute-start.24 = (bf16[256,1024]{1,0:T(8,128)(2,1)S(1)}, bf16[256,1024]{1,0:T(8,128)(2,1)S(1)}, u32[]{:S(2)}, u32[]{:S(2)}) collective-permute-start(bf16[256,1024]{1,0:T(8,128)(2,1)S(1)} %slice.225), channel_id=1, source_target_pairs={{1,0},{2,1},{3,2},{4,3},{5,4},{6,5},{7,6},{8,7},{9,8},{10,9},{11,1... | collective-permute-start | bytes 1572872 | tf_op jit(solution)/shard_map/ppermute | solution.py:23
  298.9 35.0 %collective-permute-start.25 = (bf16[64,1024]{1,0:T(8,128)(2,1)S(1)}, bf16[64,1024]{1,0:T(8,128)(2,1)S(1)}, u32[]{:S(2)}, u32[]{:S(2)}) collective-permute-start(bf16[64,1024]{1,0:T(8,128)(2,1)S(1)} %get-tuple-element.466), channel_id=1, source_target_pairs={{1,0},{2,1},{3,2},{4,3},{5,4},{6,5},{7,6},{8,7},{9,8},{10,9},{11,1... | collective-permute-start | bytes 393224 | tf_op jit(solution)/shard_map/ppermute | solution.py:23
  300.8 37.0 %collective-permute-start.26 = (bf16[64,1024]{1,0:T(8,128)(2,1)}, bf16[64,1024]{1,0:T(8,128)(2,1)}, u32[]{:S(2)}, u32[]{:S(2)}) collective-permute-start(bf16[64,1024]{1,0:T(8,128)(2,1)} %get-tuple-element.465), channel_id=1, source_target_pairs={{2,0},{3,1},{4,2},{5,3},{6,4},{7,5},{8,6},{9,7},{10,8},{11,9},{12,... | collective-permute-start | bytes 393224 | tf_op jit(solution)/shard_map/ppermute | solution.py:23
  304.8 37.8 %collective-permute-start.27 = (bf16[64,1024]{1,0:T(8,128)(2,1)S(1)}, bf16[64,1024]{1,0:T(8,128)(2,1)}, u32[]{:S(2)}, u32[]{:S(2)}) collective-permute-start(bf16[64,1024]{1,0:T(8,128)(2,1)S(1)} %get-tuple-element.464), channel_id=1, source_target_pairs={{4,0},{5,1},{6,2},{7,3},{8,4},{9,5},{10,6},{11,7},{12,8},{13,9},{1... | collective-permute-start | bytes 393224 | tf_op jit(solution)/shard_map/ppermute | solution.py:23
  308.7 17.4 %collective-permute-start.18 = (bf16[256,1024]{1,0:T(8,128)(2,1)S(1)}, bf16[256,1024]{1,0:T(8,128)(2,1)S(1)}, u32[]{:S(2)}, u32[]{:S(2)}) collective-permute-start(bf16[256,1024]{1,0:T(8,128)(2,1)S(1)} %slice.226), channel_id=1, source_target_pairs={{1,0},{2,1},{3,2},{4,3},{5,4},{6,5},{7,6},{8,7},{9,8},{10,9},{11,1... | collective-permute-start | bytes 1572872 | tf_op jit(solution)/shard_map/ppermute | solution.py:23
  313.9 34.4 %collective-permute-start.28 = (bf16[64,1024]{1,0:T(8,128)(2,1)S(1)}, bf16[64,1024]{1,0:T(8,128)(2,1)}, u32[]{:S(2)}, u32[]{:S(2)}) collective-permute-start(bf16[64,1024]{1,0:T(8,128)(2,1)S(1)} %get-tuple-element.463), channel_id=1, source_target_pairs={{8,0},{9,1},{10,2},{11,3},{12,4},{13,5},{14,6},{15,7},{16,8},{17,9... | collective-permute-start | bytes 393224 | tf_op jit(solution)/shard_map/ppermute | solution.py:23
  326.0 26.5 %collective-permute-start.19 = (bf16[64,1024]{1,0:T(8,128)(2,1)S(1)}, bf16[64,1024]{1,0:T(8,128)(2,1)}, u32[]{:S(2)}, u32[]{:S(2)}) collective-permute-start(bf16[64,1024]{1,0:T(8,128)(2,1)S(1)} %get-tuple-element.471), channel_id=1, source_target_pairs={{1,0},{2,1},{3,2},{4,3},{5,4},{6,5},{7,6},{8,7},{9,8},{10,9},{11,1... | collective-permute-start | bytes 393224 | tf_op jit(solution)/shard_map/ppermute | solution.py:23
  333.9 21.2 %collective-permute-start.20 = (bf16[64,1024]{1,0:T(8,128)(2,1)S(1)}, bf16[64,1024]{1,0:T(8,128)(2,1)}, u32[]{:S(2)}, u32[]{:S(2)}) collective-permute-start(bf16[64,1024]{1,0:T(8,128)(2,1)S(1)} %get-tuple-element.470), channel_id=1, source_target_pairs={{2,0},{3,1},{4,2},{5,3},{6,4},{7,5},{8,6},{9,7},{10,8},{11,9},{12,... | collective-permute-start | bytes 393224 | tf_op jit(solution)/shard_map/ppermute | solution.py:23
  337.7 18.7 %collective-permute-start.21 = (bf16[64,1024]{1,0:T(8,128)(2,1)S(1)}, bf16[64,1024]{1,0:T(8,128)(2,1)}, u32[]{:S(2)}, u32[]{:S(2)}) collective-permute-start(bf16[64,1024]{1,0:T(8,128)(2,1)S(1)} %get-tuple-element.469), channel_id=1, source_target_pairs={{4,0},{5,1},{6,2},{7,3},{8,4},{9,5},{10,6},{11,7},{12,8},{13,9},{1... | collective-permute-start | bytes 393224 | tf_op jit(solution)/shard_map/ppermute | solution.py:23
  342.6 15.2 %collective-permute-start.22 = (bf16[64,1024]{1,0:T(8,128)(2,1)S(1)}, bf16[64,1024]{1,0:T(8,128)(2,1)S(1)}, u32[]{:S(2)}, u32[]{:S(2)}) collective-permute-start(bf16[64,1024]{1,0:T(8,128)(2,1)S(1)} %get-tuple-element.468), channel_id=1, source_target_pairs={{8,0},{9,1},{10,2},{11,3},{12,4},{13,5},{14,6},{15,7},{16,8},{17,9... | collective-permute-start | bytes 393224 | tf_op jit(solution)/shard_map/ppermute | solution.py:23
  348.3 9.9 %collective-permute-start.23 = (bf16[64,1024]{1,0:T(8,128)(2,1)S(1)}, bf16[64,1024]{1,0:T(8,128)(2,1)S(1)}, u32[]{:S(2)}, u32[]{:S(2)}) collective-permute-start(bf16[64,1024]{1,0:T(8,128)(2,1)S(1)} %get-tuple-element.467), channel_id=1, source_target_pairs={{16,0},{17,1},{18,2},{19,3},{20,4},{21,5},{22,6},{23,7},{24,8},{25... | collective-permute-start | bytes 393224 | tf_op jit(solution)/shard_map/ppermute | solution.py:23
  352.5 5.6 %collective-permute-start.29 = (bf16[64,1024]{1,0:T(8,128)(2,1)S(1)}, bf16[64,1024]{1,0:T(8,128)(2,1)S(1)}, u32[]{:S(2)}, u32[]{:S(2)}) collective-permute-start(bf16[64,1024]{1,0:T(8,128)(2,1)S(1)} %get-tuple-element.462), channel_id=1, source_target_pairs={{16,0},{17,1},{18,2},{19,3},{20,4},{21,5},{22,6},{23,7},{24,8},{25... | collective-permute-start | bytes 393224 | tf_op jit(solution)/shard_map/ppermute | solution.py:23
  (69 other events, 356.6 us)
where the time goes:
time: 371 us; the launch traced here: 365 us
  local copies, waits for them, and re-layouts  98.8 us (27%)
  starting transfers between devices  93.9 us (25%)
  matrix products  92 us (25%)
  waiting for transfers between devices  35.3 us (10%)
  other arithmetic  32.8 us (9%)
  between operations  11.1 us (3%)
    ppermute x30, starting transfers between devices, passed_along(): lax.ppermute(value, axis, [(source, source + steps) for source in range(i...  93.9 us
    ppermute x30, waiting for transfers between devices, passed_along(): lax.ppermute(value, axis, [(source, source + steps) for source in range(i...  35.3 us
    dynamic_update_slice x36, local copies, waits for them, and re-layouts, one_group(): lax.dynamic_update_slice_in_dim(full_array, new_part, column, 1)  33.6 us
    dot_general x4, matrix products, attend_group(): jnp.einsum('hqk,khd->qhd', near_rounded, value_heads, preferred_element_t...  24 us
    dynamic_slice x32, local copies, waits for them, and re-layouts, columns_of(): return lax.dynamic_slice_in_dim(array, column, column_width, 1)  22.8 us
    dot_general x4, matrix products, attend_group(): jnp.einsum('qhd,khd->hqk', grad_heads, value_heads, preferred_element_typ...  19.5 us
    dot_general x4, matrix products, attend_group(): jnp.einsum('hqk,qhd->khd', near_rounded, grad_heads, preferred_element_ty...  17.6 us
    dynamic_update_slice x10, local copies, waits for them, and re-layouts, add_block(): lax.dynamic_update_slice_in_dim(totals, current + arrived.astype(jnp.floa...  10.9 us
  transfers between devices with their start and end apart: 30, of which 6 were waited for; matrix products, arithmetic and copies ran while one was open for 10% of the time, Pallas kernels for 0%

commit v1 on v0

v1 whole, which is shorter than its diff:
```python
import functools

import jax
import jax.numpy as jnp
from jax import lax
from jax.experimental import pallas as pl
from jax.experimental.pallas import tpu as pltpu
from jax.sharding import PartitionSpec as P

WIN = 256
BLK = 64
ROWS = 128
LANES = 128
DEAD = -1e30
CHUNKS = 2
AXES = ("grp", "seq")
F32 = jnp.float32
BF16 = jnp.bfloat16


def passed_along(value, axis, steps):
    count = lax.axis_size(axis)
    initial, last = (max(0, -steps), min(count, count - steps))
    return lax.ppermute(value, axis, [(source, source + steps) for source in range(initial, last)])


def nt(a, b):
    return lax.dot_general(a, b, (((1,), (1,)), ((), ())), preferred_element_type=F32)


def nn(a, b):
    return lax.dot_general(a, b, (((1,), (0,)), ((), ())), preferred_element_type=F32)


def block_rows_of(start, rows):
    t = lax.broadcasted_iota(jnp.int32, (BLK, rows), 0)
    j = lax.broadcasted_iota(jnp.int32, (BLK, rows), 1)
    return (j - t == start).astype(F32).astype(BF16)


def prep_kernel(levels, width, starts, ids, table, k, v, *refs):
    bias, padded = refs[0], refs[-1]
    payloads = refs[1:-1]
    rows = k.shape[0]
    types, heads = table.shape
    padded[...] = jnp.zeros_like(padded)
    padded[:, :heads] = table[...].astype(BF16).astype(F32)
    kind = lax.broadcasted_iota(jnp.int32, (types, rows), 0)
    onehot = (kind == ids[...]).astype(F32).astype(BF16)
    bias[...] = lax.dot_general(
        onehot, padded[...].astype(BF16), (((0,), (0,)), ((), ())), preferred_element_type=F32
    ).astype(BF16)
    for e in range(levels):
        pick = block_rows_of(starts[0, e], rows)
        bias_block = nn(pick, bias[...]).astype(BF16)
        for c in range(CHUNKS):
            out = payloads[c * levels + e]
            cols = slice(c * width, (c + 1) * width)
            out[0:BLK, 0:width] = nn(pick, k[:, cols]).astype(BF16)
            out[0:BLK, width : 2 * width] = nn(pick, v[:, cols]).astype(BF16)
            out[0:BLK, 2 * width :] = bias_block
            if e == 0:
                out[BLK:, 0:width] = k[rows - WIN :, cols]
                out[BLK:, width : 2 * width] = v[rows - WIN :, cols]
                out[BLK:, 2 * width :] = bias[rows - WIN :, :]


def merged(pair):
    half = LANES // 2
    return jnp.concatenate([pair[:half, :ROWS], pair[half:, ROWS:]], axis=0)


def attend_pair(head, scale, q, do, near_k, near_v, far_k, far_v, near_kt, near_vt, far_kt, far_vt,
                dot, out, dq, near_dk, near_dv, far_dk, far_dv):
    rows = q.shape[0]
    half = LANES // 2
    lane = lax.broadcasted_iota(jnp.int32, (ROWS, LANES), 1)
    first = lane < half
    ones = jnp.concatenate([(lane == head).astype(F32), (lane == head + 1).astype(F32)], axis=0)
    ones = ones.astype(BF16)
    span_row = lax.broadcasted_iota(jnp.int32, (ROWS, 2 * ROWS), 0)
    query_col = lax.broadcasted_iota(jnp.int32, (ROWS, 2 * ROWS), 1) & (ROWS - 1)
    below, above = span_row >= query_col, span_row <= query_col
    span = WIN + ROWS
    zero = jnp.zeros((ROWS, LANES), BF16)
    near_dk[...] = jnp.zeros_like(near_dk)
    near_dv[...] = jnp.zeros_like(near_dv)
    for b in range(rows // ROWS):
        mine = slice(b * ROWS, (b + 1) * ROWS)
        seen = slice(b * ROWS, b * ROWS + span)
        qb = (q[mine, :].astype(F32) * scale).astype(BF16)
        db = do[mine, :]
        q2 = jnp.concatenate([jnp.where(first, qb, zero), jnp.where(first, zero, qb)], axis=0)
        d2 = jnp.concatenate([jnp.where(first, db, zero), jnp.where(first, zero, db)], axis=0)
        qc = jnp.concatenate([q2, ones], axis=1)
        sn = nt(near_k[seen, :], qc)
        sf = nt(far_k[...], qc)
        sn = jnp.concatenate(
            [
                jnp.where(below, sn[:ROWS], DEAD),
                sn[ROWS:WIN],
                jnp.where(above, sn[WIN:], DEAD),
            ],
            axis=0,
        )
        top = jnp.maximum(jnp.max(sn, axis=0, keepdims=True), jnp.max(sf, axis=0, keepdims=True))
        en = jnp.exp(sn - top)
        ef = jnp.exp(sf - top)
        total = jnp.sum(en, axis=0, keepdims=True) + jnp.sum(ef, axis=0, keepdims=True)
        share = 1.0 / total
        wn, wf = en * share, ef * share
        rn, rf = wn.astype(BF16), wf.astype(BF16)
        att = merged(nn(near_vt[:, seen], rn) + nn(far_vt[...], rf))
        out[mine, :] = att.T.astype(out.dtype)
        parts = att * dot[:, mine]
        row_dot = jnp.concatenate(
            [
                jnp.sum(parts[:half], axis=0, keepdims=True),
                jnp.sum(parts[half:], axis=0, keepdims=True),
            ],
            axis=1,
        )
        gn = (wn * (nt(near_v[seen, :], d2) - row_dot)).astype(BF16)
        gf = (wf * (nt(far_v[...], d2) - row_dot)).astype(BF16)
        dqt = merged(nn(near_kt[:, seen], gn) + nn(far_kt[...], gf)) * scale
        dq[mine, :] = dqt.T.astype(dq.dtype)
        near_dk[seen, :] += nn(gn, q2)
        near_dv[seen, :] += nn(rn, d2)
        if b == 0:
            far_dk[...] = nn(gf, q2)
            far_dv[...] = nn(rf, d2)
        else:
            far_dk[...] += nn(gf, q2)
            far_dv[...] += nn(rf, d2)


def load_pair(levels, position, column, k, v, bias, payload_of, near_k, near_v, far_k, far_v,
              near_kt, near_vt, far_kt, far_vt, dot, do):
    near_k[WIN:, :LANES] = k[...]
    near_k[WIN:, LANES:] = bias[...]
    near_v[WIN:, :] = v[...]
    for e in range(levels):
        keys, values, biases = payload_of(e)
        biases = jnp.where(position >= 2**e, biases, jnp.full_like(biases, DEAD))
        at = slice(e * BLK, (e + 1) * BLK)
        far_k[at, :LANES] = keys[:BLK]
        far_k[at, LANES:] = biases[:BLK]
        far_v[at, :] = values[:BLK]
        if e == 0:
            near_k[:WIN, :LANES] = keys[BLK:]
            near_k[:WIN, LANES:] = biases[BLK:]
            near_v[:WIN, :] = values[BLK:]
    near_kt[...] = near_k[:, :LANES].T
    near_vt[...] = near_v[...].T
    far_kt[...] = far_k[:, :LANES].T
    far_vt[...] = far_v[...].T
    dot[...] = do[...].astype(F32).T


def attend_kernel(levels, base, scale, place, q, k, v, do, bias, *refs):
    payloads = refs[: 3 * levels]
    out, dq, own_dk, own_dv = refs[3 * levels : 3 * levels + 4]
    back = refs[3 * levels + 4 : 3 * levels + 4 + 2 * levels]
    (near_k, near_v, far_k, far_v, near_kt, near_vt, far_kt, far_vt, dot, near_dk, near_dv,
     far_dk, far_dv) = refs[3 * levels + 4 + 2 * levels :]
    position = place[0]
    load_pair(
        levels, position, 0, k, v, bias,
        lambda e: tuple(payloads[3 * e + i][...] for i in range(3)),
        near_k, near_v, far_k, far_v, near_kt, near_vt, far_kt, far_vt, dot, do,
    )
    head = 2 * (base + pl.program_id(0))
    attend_pair(head, scale, q, do, near_k, near_v, far_k, far_v, near_kt, near_vt, far_kt,
                far_vt, dot, out, dq, near_dk, near_dv, far_dk, far_dv)
    own_dk[...] = near_dk[WIN:, :]
    own_dv[...] = near_dv[WIN:, :]
    for e in range(levels):
        at = slice(e * BLK, (e + 1) * BLK)
        for ref, far, near in ((back[2 * e], far_dk, near_dk), (back[2 * e + 1], far_dv, near_dv)):
            ref[:BLK, :] = far[at, :].astype(BF16)
            if e == 0:
                ref[BLK:, :] = near[:WIN, :].astype(BF16)


def settle_kernel(levels, starts, own_dk, own_dv, *refs):
    back = refs[: 2 * levels]
    dk, dv = refs[2 * levels :]
    rows = own_dk.shape[0]
    for which, own, final in ((0, own_dk, dk), (1, own_dv, dv)):
        total = own[...]
        for e in range(levels):
            place = block_rows_of(starts[0, e], rows)
            arrived = back[2 * e + which]
            total = total + lax.dot_general(
                place, arrived[:BLK, :], (((0,), (0,)), ((), ())), preferred_element_type=F32
            )
        first = rows - WIN
        final[:first, :] = total[:first].astype(BF16)
        final[first:, :] = (total[first:] + back[which][BLK:, :].astype(F32)).astype(BF16)


def local(queries, keys, values, event_ids, type_bias, block_start, d_out):
    rows, width_all = queries.shape
    heads = type_bias.shape[1]
    levels = block_start.shape[1]
    scale = (width_all // heads) ** -0.5
    width = width_all // CHUNKS
    pairs = width // LANES
    far = levels * BLK
    sds = jax.ShapeDtypeStruct
    smem = pl.BlockSpec(memory_space=pltpu.SMEM)
    vmem = pl.BlockSpec(memory_space=pltpu.VMEM)
    depth = [BLK + (WIN if e == 0 else 0) for e in range(levels)]
    params = pltpu.CompilerParams(vmem_limit_bytes=48 * 2**20)

    prepared = pl.pallas_call(
        functools.partial(prep_kernel, levels, width),
        out_shape=[sds((rows, LANES), BF16)]
        + [sds((depth[e], 2 * width + LANES), BF16) for _ in range(CHUNKS) for e in range(levels)],
        in_specs=[smem, vmem, vmem, vmem, vmem],
        out_specs=[vmem] * (1 + CHUNKS * levels),
        scratch_shapes=[pltpu.VMEM((type_bias.shape[0], LANES), F32)],
        compiler_params=params,
        name="prep",
    )(block_start, event_ids[None, :], type_bias, keys, values)
    bias, payloads = prepared[0], prepared[1:]
    position = lax.axis_index(AXES).astype(jnp.int32)[None]

    arrived = [
        [passed_along(payloads[c * levels + e], AXES, 2**e) for e in range(levels)]
        for c in range(CHUNKS)
    ]
    parts = []
    returned = []
    for c in range(CHUNKS):
        base = c * pairs

        def column(p, base=base):
            return (0, base + p)

        def own_column(p):
            return (0, p)

        wide = pl.BlockSpec((rows, LANES), column)
        narrow = pl.BlockSpec((rows, LANES), own_column)
        specs, operands = [], []
        for e in range(levels):
            for i in range(3):
                specs.append(
                    pl.BlockSpec(
                        (depth[e], LANES),
                        (lambda p, i=i: (0, i * pairs + p)) if i < 2 else (lambda p: (0, 2 * pairs)),
                    )
                )
                operands.append(arrived[c][e])
        cost = 12 * rows * (WIN + ROWS + far) * width
        res = pl.pallas_call(
            functools.partial(attend_kernel, levels, base, scale),
            grid=(pairs,),
            out_shape=[sds((rows, width), BF16)] * 2
            + [sds((rows, width), F32)] * 2
            + [sds((depth[e], width), BF16) for e in range(levels) for _ in range(2)],
            in_specs=[smem, wide, wide, wide, wide, pl.BlockSpec((rows, LANES), lambda p: (0, 0))]
            + specs,
            out_specs=[narrow] * 4
            + [pl.BlockSpec((depth[e], LANES), own_column) for e in range(levels) for _ in range(2)],
            scratch_shapes=[
                pltpu.VMEM((WIN + rows, 2 * LANES), BF16),
                pltpu.VMEM((WIN + rows, LANES), BF16),
                pltpu.VMEM((far, 2 * LANES), BF16),
                pltpu.VMEM((far, LANES), BF16),
                pltpu.VMEM((LANES, WIN + rows), BF16),
                pltpu.VMEM((LANES, WIN + rows), BF16),
                pltpu.VMEM((LANES, far), BF16),
                pltpu.VMEM((LANES, far), BF16),
                pltpu.VMEM((LANES, rows), F32),
                pltpu.VMEM((WIN + rows, LANES), F32),
                pltpu.VMEM((WIN + rows, LANES), F32),
                pltpu.VMEM((far, LANES), F32),
                pltpu.VMEM((far, LANES), F32),
            ],
            compiler_params=params,
            cost_estimate=pl.CostEstimate(
                flops=cost * 4, bytes_accessed=16 * rows * width, transcendentals=0
            ),
            name="attend",
        )(position, queries, keys, values, d_out, bias, *operands)
        parts.append(res[:4])
        returned.append(
            [passed_along(tuple(res[4 + 2 * e : 6 + 2 * e]), AXES, -(2**e)) for e in range(levels)]
        )
    finals = []
    for c in range(CHUNKS):
        step = min(width, 256)
        block = pl.BlockSpec((rows, step), lambda p: (0, p))
        finals.append(
            pl.pallas_call(
                functools.partial(settle_kernel, levels),
                grid=(width // step,),
                out_shape=[sds((rows, width), BF16)] * 2,
                in_specs=[smem, block, block]
                + [
                    pl.BlockSpec((depth[e], step), lambda p: (0, p))
                    for e in range(levels)
                    for _ in range(2)
                ],
                out_specs=[block] * 2,
                compiler_params=params,
                name="settle",
            )(block_start, parts[c][2], parts[c][3], *[a for pair in returned[c] for a in pair])
        )
    return tuple(
        jnp.concatenate(list(chunk), axis=1)
        for chunk in (
            [p[0] for p in parts],
            [p[1] for p in parts],
            [f[0] for f in finals],
            [f[1] for f in finals],
        )
    )


def solution(mesh):
    rows = P(AXES, None)
    return jax.shard_map(
        local,
        mesh=mesh,
        in_specs=(rows, rows, rows, P(AXES), P(), rows, rows),
        out_specs=(rows, rows, rows, rows),
        check_vma=False,
    )
```

time: 371 us -> 187 us (0.50)
  local copies, waits for them, and re-layouts: 98.8 us -> 6.21 us
  matrix products: 92 us -> 0 us
  Pallas kernels: 0 us -> 48.5 us
  other arithmetic: 32.8 us -> 3.16 us
  waiting for transfers between devices: 35.3 us -> 17 us
  starting transfers between devices: 93.9 us -> 108 us
  between operations: 11.1 us -> 1.16 us
    dot_general x49 -> x0, matrix products: 92 us -> none  [the longest x4 24 us: attend_group(): jnp.einsum('hqk,khd->qhd', near_rounded, value_heads, preferred_element_t...]
    pallas_call x0 -> x5, Pallas kernels: none -> 48.5 us  [the longest x2 39.9 us: local(): pl.pallas_call(functools.partial(attend_kernel, levels, base, scale), gri...]
    dynamic_update_slice x46 -> x0, local copies, waits for them, and re-layouts: 44.5 us -> none  [the longest x36 33.6 us: one_group(): lax.dynamic_update_slice_in_dim(full_array, new_part, column, 1)]
    dynamic_slice x35 -> x0, local copies, waits for them, and re-layouts: 25.9 us -> none  [the longest x32 22.8 us: columns_of(): return lax.dynamic_slice_in_dim(array, column, column_width, 1)]
    ppermute x30, waiting for transfers between devices: 35.3 us -> 17 us  [passed_along(): lax.ppermute(value, axis, [(source, source + steps) for source in range(i...]
    ppermute x30, starting transfers between devices: 93.9 us -> 108 us  [passed_along(): lax.ppermute(value, axis, [(source, source + steps) for source in range(i...]
    reduce_sum x8 -> x0, other arithmetic: 9.47 us -> none  [the longest x4 7.96 us: attend_group(): jnp.sum(near_exp, axis=-1, keepdims=True)]
    another operation x6 -> x0, local copies, waits for them, and re-layouts: 8.28 us -> none
  transfers between devices with their start and end apart: 30 -> 30, of which waited for: 6 -> 3; matrix products, arithmetic and copies ran while one was open for 10% -> 1% of each run, Pallas kernels for 0% -> 23%
where the time goes in v1:
time: 187 us; the launch traced here: 184 us
  starting transfers between devices  108 us (58%)
  Pallas kernels  48.5 us (26%)
  waiting for transfers between devices  17 us (9%)
  local copies, waits for them, and re-layouts  6.21 us (3%)
  other arithmetic  3.16 us (2%)
    ppermute x30, starting transfers between devices, passed_along(): lax.ppermute(value, axis, [(source, source + steps) for source in range(i...  108 us
    pallas_call x2, Pallas kernels, local(): pl.pallas_call(functools.partial(attend_kernel, levels, base, scale), gri...  39.9 us
    ppermute x30, waiting for transfers between devices, passed_along(): lax.ppermute(value, axis, [(source, source + steps) for source in range(i...  17 us
    unnamed x15, local copies, waits for them, and re-layouts  6.21 us
    pallas_call x2, Pallas kernels, local(): pl.pallas_call(functools.partial(settle_kernel, levels), grid=(width // s...  5.14 us
  transfers between devices with their start and end apart: 30, of which 3 were waited for; matrix products, arithmetic and copies ran while one was open for 1% of the time, Pallas kernels for 23%

profile of v1, /device:TPU:2, one launch (start us, length us, event | category | flops | bytes accessed | tf_op | source)
XLA Modules:
  0.0 184.4 jit_solution(16669907046193472551)
XLA Ops:
  5.3 3.5 %prep.1 = (bf16[512,128]{1,0:T(8,128)(2,1)S(1)}, bf16[320,1152]{1,0:T(8,128)(2,1)S(1)}, bf16[64,1152]{1,0:T(8,128)(2,1)}, bf16[64,1152]{1,0:T(8,128)(2,1)}, bf16...) custom-call(s32[1,5]{1,0:T(1,128)S(1)} %copy-done.2, ...), custom_call_target="tpu_custom_call" | custom-call | tf_op jit(solution)/shard_map/prep/pallas_call | solution.py:216
  9.5 3.4 %collective-permute-start = (bf16[320,1152]{1,0:T(8,128)(2,1)S(1)}, bf16[320,1152]{1,0:T(8,128)(2,1)S(1)}, u32[]{:S(2)}, u32[]{:S(2)}) collective-permute-start(bf16[320,1152]{1,0:T(8,128)(2,1)S(1)} %get-tuple-element.48), channel_id=1, source_target_pairs={{0,1},{1,2},{2,3},{3,4},{4,5},{5,6},{6,7},{7,8},{8,9},{9,10},{10,1... | collective-permute-start | bytes 2211848 | tf_op jit(solution)/shard_map/ppermute | solution.py:24
  12.9 3.5 %collective-permute-start.1 = (bf16[64,1152]{1,0:T(8,128)(2,1)}, bf16[64,1152]{1,0:T(8,128)(2,1)S(1)}, u32[]{:S(2)}, u32[]{:S(2)}) collective-permute-start(bf16[64,1152]{1,0:T(8,128)(2,1)} %get-tuple-element.49), channel_id=1, source_target_pairs={{0,2},{1,3},{2,4},{3,5},{4,6},{5,7},{6,8},{7,9},{8,10},{9,11},{10,... | collective-permute-start | bytes 442376 | tf_op jit(solution)/shard_map/ppermute | solution.py:24
  16.4 4.5 %collective-permute-start.2 = (bf16[64,1152]{1,0:T(8,128)(2,1)}, bf16[64,1152]{1,0:T(8,128)(2,1)S(1)}, u32[]{:S(2)}, u32[]{:S(2)}) collective-permute-start(bf16[64,1152]{1,0:T(8,128)(2,1)} %get-tuple-element.50), channel_id=1, source_target_pairs={{0,4},{1,5},{2,6},{3,7},{4,8},{5,9},{6,10},{7,11},{8,12},{9,13},{1... | collective-permute-start | bytes 442376 | tf_op jit(solution)/shard_map/ppermute | solution.py:24
  20.9 1.9 %collective-permute-start.3 = (bf16[64,1152]{1,0:T(8,128)(2,1)}, bf16[64,1152]{1,0:T(8,128)(2,1)S(1)}, u32[]{:S(2)}, u32[]{:S(2)}) collective-permute-start(bf16[64,1152]{1,0:T(8,128)(2,1)} %get-tuple-element.51), channel_id=1, source_target_pairs={{0,8},{1,9},{2,10},{3,11},{4,12},{5,13},{6,14},{7,15},{8,16},{9,17... | collective-permute-start | bytes 442376 | tf_op jit(solution)/shard_map/ppermute | solution.py:24
  24.1 15.2 %collective-permute-start.5 = (bf16[320,1152]{1,0:T(8,128)(2,1)S(1)}, bf16[320,1152]{1,0:T(8,128)(2,1)S(1)}, u32[]{:S(2)}, u32[]{:S(2)}) collective-permute-start(bf16[320,1152]{1,0:T(8,128)(2,1)S(1)} %get-tuple-element.54), channel_id=1, source_target_pairs={{0,1},{1,2},{2,3},{3,4},{4,5},{5,6},{6,7},{7,8},{8,9},{9,10},{10,1... | collective-permute-start | bytes 2211848 | tf_op jit(solution)/shard_map/ppermute | solution.py:24
  39.4 3.3 %collective-permute-start.6 = (bf16[64,1152]{1,0:T(8,128)(2,1)S(1)}, bf16[64,1152]{1,0:T(8,128)(2,1)S(1)}, u32[]{:S(2)}, u32[]{:S(2)}) collective-permute-start(bf16[64,1152]{1,0:T(8,128)(2,1)S(1)} %get-tuple-element.55), channel_id=1, source_target_pairs={{0,2},{1,3},{2,4},{3,5},{4,6},{5,7},{6,8},{7,9},{8,10},{9,11},{10,... | collective-permute-start | bytes 442376 | tf_op jit(solution)/shard_map/ppermute | solution.py:24
  42.7 4.1 %collective-permute-start.7 = (bf16[64,1152]{1,0:T(8,128)(2,1)S(1)}, bf16[64,1152]{1,0:T(8,128)(2,1)S(1)}, u32[]{:S(2)}, u32[]{:S(2)}) collective-permute-start(bf16[64,1152]{1,0:T(8,128)(2,1)S(1)} %get-tuple-element.56), channel_id=1, source_target_pairs={{0,4},{1,5},{2,6},{3,7},{4,8},{5,9},{6,10},{7,11},{8,12},{9,13},{1... | collective-permute-start | bytes 442376 | tf_op jit(solution)/shard_map/ppermute | solution.py:24
  46.9 1.9 %collective-permute-start.8 = (bf16[64,1152]{1,0:T(8,128)(2,1)S(1)}, bf16[64,1152]{1,0:T(8,128)(2,1)S(1)}, u32[]{:S(2)}, u32[]{:S(2)}) collective-permute-start(bf16[64,1152]{1,0:T(8,128)(2,1)S(1)} %get-tuple-element.57), channel_id=1, source_target_pairs={{0,8},{1,9},{2,10},{3,11},{4,12},{5,13},{6,14},{7,15},{8,16},{9,17... | collective-permute-start | bytes 442376 | tf_op jit(solution)/shard_map/ppermute | solution.py:24
  51.0 19.9 %attend.2 = (bf16[512,512]{1,0:T(8,128)(2,1)S(1)}, bf16[512,512]{1,0:T(8,128)(2,1)S(1)}, f32[512,512]{1,0:T(8,128)S(1)}, f32[512,512]{1,0:T(8,128)S(1)}, bf16[32...) custom-call(s32[1]{0:T(128)} %bitcast.place, ...), custom_call_target="tpu_custom_call" | custom-call | flops 8858370048 | bytes 4194304 | tf_op jit(solution)/shard_map/attend/pallas_call | solution.py:257
  70.9 5.5 %collective-permute-start.12 = (bf16[64,512]{1,0:T(8,128)(2,1)S(1)}, bf16[64,512]{1,0:T(8,128)(2,1)S(1)}, u32[]{:S(2)}, u32[]{:S(2)}) collective-permute-start(bf16[64,512]{1,0:T(8,128)(2,1)S(1)} %get-tuple-element.66), channel_id=1, source_target_pairs={{2,0},{3,1},{4,2},{5,3},{6,4},{7,5},{8,6},{9,7},{10,8},{11,9},{12,... | collective-permute-start | bytes 196616 | tf_op jit(solution)/shard_map/ppermute | solution.py:24
  76.4 1.9 %collective-permute-start.13 = (bf16[64,512]{1,0:T(8,128)(2,1)S(1)}, bf16[64,512]{1,0:T(8,128)(2,1)S(1)}, u32[]{:S(2)}, u32[]{:S(2)}) collective-permute-start(bf16[64,512]{1,0:T(8,128)(2,1)S(1)} %get-tuple-element.67), channel_id=1, source_target_pairs={{2,0},{3,1},{4,2},{5,3},{6,4},{7,5},{8,6},{9,7},{10,8},{11,9},{12,... | collective-permute-start | bytes 196616 | tf_op jit(solution)/shard_map/ppermute | solution.py:24
  78.4 2.5 %collective-permute-start.14 = (bf16[64,512]{1,0:T(8,128)(2,1)S(1)}, bf16[64,512]{1,0:T(8,128)(2,1)S(1)}, u32[]{:S(2)}, u32[]{:S(2)}) collective-permute-start(bf16[64,512]{1,0:T(8,128)(2,1)S(1)} %get-tuple-element.68), channel_id=1, source_target_pairs={{4,0},{5,1},{6,2},{7,3},{8,4},{9,5},{10,6},{11,7},{12,8},{13,9},{1... | collective-permute-start | bytes 196616 | tf_op jit(solution)/shard_map/ppermute | solution.py:24
  80.8 4.1 %collective-permute-start.15 = (bf16[64,512]{1,0:T(8,128)(2,1)S(1)}, bf16[64,512]{1,0:T(8,128)(2,1)S(1)}, u32[]{:S(2)}, u32[]{:S(2)}) collective-permute-start(bf16[64,512]{1,0:T(8,128)(2,1)S(1)} %get-tuple-element.69), channel_id=1, source_target_pairs={{4,0},{5,1},{6,2},{7,3},{8,4},{9,5},{10,6},{11,7},{12,8},{13,9},{1... | collective-permute-start | bytes 196616 | tf_op jit(solution)/shard_map/ppermute | solution.py:24
  85.0 1.9 %collective-permute-start.16 = (bf16[64,512]{1,0:T(8,128)(2,1)S(1)}, bf16[64,512]{1,0:T(8,128)(2,1)S(1)}, u32[]{:S(2)}, u32[]{:S(2)}) collective-permute-start(bf16[64,512]{1,0:T(8,128)(2,1)S(1)} %get-tuple-element.70), channel_id=1, source_target_pairs={{8,0},{9,1},{10,2},{11,3},{12,4},{13,5},{14,6},{15,7},{16,8},{17,9... | collective-permute-start | bytes 196616 | tf_op jit(solution)/shard_map/ppermute | solution.py:24
  86.9 21.5 %collective-permute-start.10 = (bf16[320,512]{1,0:T(8,128)(2,1)S(1)}, bf16[320,512]{1,0:T(8,128)(2,1)S(1)}, u32[]{:S(2)}, u32[]{:S(2)}) collective-permute-start(bf16[320,512]{1,0:T(8,128)(2,1)S(1)} %get-tuple-element.64), channel_id=1, source_target_pairs={{1,0},{2,1},{3,2},{4,3},{5,4},{6,5},{7,6},{8,7},{9,8},{10,9},{11,1... | collective-permute-start | bytes 983048 | tf_op jit(solution)/shard_map/ppermute | solution.py:24
  108.4 1.9 %collective-permute-start.11 = (bf16[320,512]{1,0:T(8,128)(2,1)S(1)}, bf16[320,512]{1,0:T(8,128)(2,1)S(1)}, u32[]{:S(2)}, u32[]{:S(2)}) collective-permute-start(bf16[320,512]{1,0:T(8,128)(2,1)S(1)} %get-tuple-element.65), channel_id=1, source_target_pairs={{1,0},{2,1},{3,2},{4,3},{5,4},{6,5},{7,6},{8,7},{9,8},{10,9},{11,1... | collective-permute-start | bytes 983048 | tf_op jit(solution)/shard_map/ppermute | solution.py:24
  110.4 1.9 %collective-permute-start.17 = (bf16[64,512]{1,0:T(8,128)(2,1)S(1)}, bf16[64,512]{1,0:T(8,128)(2,1)S(1)}, u32[]{:S(2)}, u32[]{:S(2)}) collective-permute-start(bf16[64,512]{1,0:T(8,128)(2,1)S(1)} %get-tuple-element.71), channel_id=1, source_target_pairs={{8,0},{9,1},{10,2},{11,3},{12,4},{13,5},{14,6},{15,7},{16,8},{17,9... | collective-permute-start | bytes 196616 | tf_op jit(solution)/shard_map/ppermute | solution.py:24
  114.9 20.0 %attend.3 = (bf16[512,512]{1,0:T(8,128)(2,1)S(1)}, bf16[512,512]{1,0:T(8,128)(2,1)S(1)}, f32[512,512]{1,0:T(8,128)S(1)}, f32[512,512]{1,0:T(8,128)S(1)}, bf16[32...) custom-call(s32[1]{0:T(128)} %bitcast.place, ...), custom_call_target="tpu_custom_call" | custom-call | flops 8858370048 | bytes 4194304 | tf_op jit(solution)/shard_map/attend/pallas_call | solution.py:257
  134.9 1.9 %collective-permute-start.22 = (bf16[64,512]{1,0:T(8,128)(2,1)S(1)}, bf16[64,512]{1,0:T(8,128)(2,1)S(1)}, u32[]{:S(2)}, u32[]{:S(2)}) collective-permute-start(bf16[64,512]{1,0:T(8,128)(2,1)S(1)} %get-tuple-element.79), channel_id=1, source_target_pairs={{2,0},{3,1},{4,2},{5,3},{6,4},{7,5},{8,6},{9,7},{10,8},{11,9},{12,... | collective-permute-start | bytes 196616 | tf_op jit(solution)/shard_map/ppermute | solution.py:24
  136.8 2.2 %collective-permute-start.23 = (bf16[64,512]{1,0:T(8,128)(2,1)S(1)}, bf16[64,512]{1,0:T(8,128)(2,1)S(1)}, u32[]{:S(2)}, u32[]{:S(2)}) collective-permute-start(bf16[64,512]{1,0:T(8,128)(2,1)S(1)} %get-tuple-element.80), channel_id=1, source_target_pairs={{2,0},{3,1},{4,2},{5,3},{6,4},{7,5},{8,6},{9,7},{10,8},{11,9},{12,... | collective-permute-start | bytes 196616 | tf_op jit(solution)/shard_map/ppermute | solution.py:24
  139.1 1.9 %collective-permute-start.24 = (bf16[64,512]{1,0:T(8,128)(2,1)S(1)}, bf16[64,512]{1,0:T(8,128)(2,1)S(1)}, u32[]{:S(2)}, u32[]{:S(2)}) collective-permute-start(bf16[64,512]{1,0:T(8,128)(2,1)S(1)} %get-tuple-element.81), channel_id=1, source_target_pairs={{4,0},{5,1},{6,2},{7,3},{8,4},{9,5},{10,6},{11,7},{12,8},{13,9},{1... | collective-permute-start | bytes 196616 | tf_op jit(solution)/shard_map/ppermute | solution.py:24
  141.3 5.9 %collective-permute-start.20 = (bf16[320,512]{1,0:T(8,128)(2,1)S(1)}, bf16[320,512]{1,0:T(8,128)(2,1)S(1)}, u32[]{:S(2)}, u32[]{:S(2)}) collective-permute-start(bf16[320,512]{1,0:T(8,128)(2,1)S(1)} %get-tuple-element.77), channel_id=1, source_target_pairs={{1,0},{2,1},{3,2},{4,3},{5,4},{6,5},{7,6},{8,7},{9,8},{10,9},{11,1... | collective-permute-start | bytes 983048 | tf_op jit(solution)/shard_map/ppermute | solution.py:24
  147.3 1.9 %collective-permute-start.21 = (bf16[320,512]{1,0:T(8,128)(2,1)S(1)}, bf16[320,512]{1,0:T(8,128)(2,1)S(1)}, u32[]{:S(2)}, u32[]{:S(2)}) collective-permute-start(bf16[320,512]{1,0:T(8,128)(2,1)S(1)} %get-tuple-element.78), channel_id=1, source_target_pairs={{1,0},{2,1},{3,2},{4,3},{5,4},{6,5},{7,6},{8,7},{9,8},{10,9},{11,1... | collective-permute-start | bytes 983048 | tf_op jit(solution)/shard_map/ppermute | solution.py:24
  149.2 1.9 %collective-permute-start.25 = (bf16[64,512]{1,0:T(8,128)(2,1)S(1)}, bf16[64,512]{1,0:T(8,128)(2,1)S(1)}, u32[]{:S(2)}, u32[]{:S(2)}) collective-permute-start(bf16[64,512]{1,0:T(8,128)(2,1)S(1)} %get-tuple-element.82), channel_id=1, source_target_pairs={{4,0},{5,1},{6,2},{7,3},{8,4},{9,5},{10,6},{11,7},{12,8},{13,9},{1... | collective-permute-start | bytes 196616 | tf_op jit(solution)/shard_map/ppermute | solution.py:24
  151.1 14.8 %collective-permute-done.25.refs_5_ = bf16[64,512]{1,0:T(8,128)(2,1)S(1)} collective-permute-done((bf16[64,512]{1,0:T(8,128)(2,1)S(1)}, bf16[64,512]{1,0:T(8,128)(2,1)S(1)}, u32[]{:S(2)}, u32[]{:S(2)}) %collective-permute-start.25) | collective-permute-done | bytes 65568 | tf_op jit(solution)/shard_map/ppermute | solution.py:24
  165.9 1.9 %collective-permute-start.26 = (bf16[64,512]{1,0:T(8,128)(2,1)S(1)}, bf16[64,512]{1,0:T(8,128)(2,1)S(1)}, u32[]{:S(2)}, u32[]{:S(2)}) collective-permute-start(bf16[64,512]{1,0:T(8,128)(2,1)S(1)} %get-tuple-element.83), channel_id=1, source_target_pairs={{8,0},{9,1},{10,2},{11,3},{12,4},{13,5},{14,6},{15,7},{16,8},{17,9... | collective-permute-start | bytes 196616 | tf_op jit(solution)/shard_map/ppermute | solution.py:24
  167.8 1.9 %collective-permute-done.26.refs_6_ = bf16[64,512]{1,0:T(8,128)(2,1)S(1)} collective-permute-done((bf16[64,512]{1,0:T(8,128)(2,1)S(1)}, bf16[64,512]{1,0:T(8,128)(2,1)S(1)}, u32[]{:S(2)}, u32[]{:S(2)}) %collective-permute-start.26) | collective-permute-done | bytes 65568 | tf_op jit(solution)/shard_map/ppermute | solution.py:24
  169.7 3.7 %collective-permute-start.27 = (bf16[64,512]{1,0:T(8,128)(2,1)S(1)}, bf16[64,512]{1,0:T(8,128)(2,1)S(1)}, u32[]{:S(2)}, u32[]{:S(2)}) collective-permute-start(bf16[64,512]{1,0:T(8,128)(2,1)S(1)} %get-tuple-element.84), channel_id=1, source_target_pairs={{8,0},{9,1},{10,2},{11,3},{12,4},{13,5},{14,6},{15,7},{16,8},{17,9... | collective-permute-start | bytes 196616 | tf_op jit(solution)/shard_map/ppermute | solution.py:24
  176.0 1.6 pad_maximum_fusion
  177.6 2.6 %settle.2 = (bf16[512,512]{1,0:T(8,128)(2,1)S(1)}, bf16[512,512]{1,0:T(8,128)(2,1)S(1)}) custom-call(s32[1,5]{1,0:T(1,128)S(1)} %copy-done.3, f32[512,512]{1,0:T(8,128)S(1)} %get-tuple-element.62.own_dk, f32[512,512]{1,0:T(8,128)S(1)} %get-tuple-element.63.own_dv, bf16[320,512]{1,0:T(8,128)(2,1)S(1)} %collective-permute-done.10.refs_0_, ...), custom_call_target="tpu_custom_call" | custom-call | tf_op jit(solution)/shard_map/settle/pallas_call | solution.py:297
  180.2 2.6 %settle.3 = (bf16[512,512]{1,0:T(8,128)(2,1)S(1)}, bf16[512,512]{1,0:T(8,128)(2,1)S(1)}) custom-call(s32[1,5]{1,0:T(1,128)S(1)} %copy-done.3, f32[512,512]{1,0:T(8,128)S(1)} %get-tuple-element.75.own_dk, f32[512,512]{1,0:T(8,128)S(1)} %get-tuple-element.76.own_dv, bf16[320,512]{1,0:T(8,128)(2,1)S(1)} %collective-permute-done.20.refs_0_, ...), custom_call_target="tpu_custom_call" | custom-call | tf_op jit(solution)/shard_map/settle/pallas_call | solution.py:297
  (50 shorter events, 15.9 us)
Async XLA Ops:
  1.5 1.2 copy-start
  9.5 39.3 %collective-permute-start = (bf16[320,1152]{1,0:T(8,128)(2,1)S(1)}, bf16[320,1152]{1,0:T(8,128)(2,1)S(1)}, u32[]{:S(2)}, u32[]{:S(2)}) collective-permute-start(bf16[320,1152]{1,0:T(8,128)(2,1)S(1)} %get-tuple-element.48), channel_id=1, source_target_pairs={{0,1},{1,2},{2,3},{3,4},{4,5},{5,6},{6,7},{7,8},{8,9},{9,10},{10,1... | collective-permute-start | bytes 2211848 | tf_op jit(solution)/shard_map/ppermute | solution.py:24
  12.9 11.2 %collective-permute-start.1 = (bf16[64,1152]{1,0:T(8,128)(2,1)}, bf16[64,1152]{1,0:T(8,128)(2,1)S(1)}, u32[]{:S(2)}, u32[]{:S(2)}) collective-permute-start(bf16[64,1152]{1,0:T(8,128)(2,1)} %get-tuple-element.49), channel_id=1, source_target_pairs={{0,2},{1,3},{2,4},{3,5},{4,6},{5,7},{6,8},{7,9},{8,10},{9,11},{10,... | collective-permute-start | bytes 442376 | tf_op jit(solution)/shard_map/ppermute | solution.py:24
  16.4 23.0 %collective-permute-start.2 = (bf16[64,1152]{1,0:T(8,128)(2,1)}, bf16[64,1152]{1,0:T(8,128)(2,1)S(1)}, u32[]{:S(2)}, u32[]{:S(2)}) collective-permute-start(bf16[64,1152]{1,0:T(8,128)(2,1)} %get-tuple-element.50), channel_id=1, source_target_pairs={{0,4},{1,5},{2,6},{3,7},{4,8},{5,9},{6,10},{7,11},{8,12},{9,13},{1... | collective-permute-start | bytes 442376 | tf_op jit(solution)/shard_map/ppermute | solution.py:24
  20.9 21.8 %collective-permute-start.3 = (bf16[64,1152]{1,0:T(8,128)(2,1)}, bf16[64,1152]{1,0:T(8,128)(2,1)S(1)}, u32[]{:S(2)}, u32[]{:S(2)}) collective-permute-start(bf16[64,1152]{1,0:T(8,128)(2,1)} %get-tuple-element.51), channel_id=1, source_target_pairs={{0,8},{1,9},{2,10},{3,11},{4,12},{5,13},{6,14},{7,15},{8,16},{9,17... | collective-permute-start | bytes 442376 | tf_op jit(solution)/shard_map/ppermute | solution.py:24
  22.8 24.1 %collective-permute-start.4 = (bf16[64,1152]{1,0:T(8,128)(2,1)}, bf16[64,1152]{1,0:T(8,128)(2,1)S(1)}, u32[]{:S(2)}, u32[]{:S(2)}) collective-permute-start(bf16[64,1152]{1,0:T(8,128)(2,1)} %get-tuple-element.52), channel_id=1, source_target_pairs={{0,16},{1,17},{2,18},{3,19},{4,20},{5,21},{6,22},{7,23},{8,24},{9,... | collective-permute-start | bytes 442376 | tf_op jit(solution)/shard_map/ppermute | solution.py:24
  24.1 60.8 %collective-permute-start.5 = (bf16[320,1152]{1,0:T(8,128)(2,1)S(1)}, bf16[320,1152]{1,0:T(8,128)(2,1)S(1)}, u32[]{:S(2)}, u32[]{:S(2)}) collective-permute-start(bf16[320,1152]{1,0:T(8,128)(2,1)S(1)} %get-tuple-element.54), channel_id=1, source_target_pairs={{0,1},{1,2},{2,3},{3,4},{4,5},{5,6},{6,7},{7,8},{8,9},{9,10},{10,1... | collective-permute-start | bytes 2211848 | tf_op jit(solution)/shard_map/ppermute | solution.py:24
  39.4 31.5 %collective-permute-start.6 = (bf16[64,1152]{1,0:T(8,128)(2,1)S(1)}, bf16[64,1152]{1,0:T(8,128)(2,1)S(1)}, u32[]{:S(2)}, u32[]{:S(2)}) collective-permute-start(bf16[64,1152]{1,0:T(8,128)(2,1)S(1)} %get-tuple-element.55), channel_id=1, source_target_pairs={{0,2},{1,3},{2,4},{3,5},{4,6},{5,7},{6,8},{7,9},{8,10},{9,11},{10,... | collective-permute-start | bytes 442376 | tf_op jit(solution)/shard_map/ppermute | solution.py:24
  42.7 33.7 %collective-permute-start.7 = (bf16[64,1152]{1,0:T(8,128)(2,1)S(1)}, bf16[64,1152]{1,0:T(8,128)(2,1)S(1)}, u32[]{:S(2)}, u32[]{:S(2)}) collective-permute-start(bf16[64,1152]{1,0:T(8,128)(2,1)S(1)} %get-tuple-element.56), channel_id=1, source_target_pairs={{0,4},{1,5},{2,6},{3,7},{4,8},{5,9},{6,10},{7,11},{8,12},{9,13},{1... | collective-permute-start | bytes 442376 | tf_op jit(solution)/shard_map/ppermute | solution.py:24
  46.9 31.5 %collective-permute-start.8 = (bf16[64,1152]{1,0:T(8,128)(2,1)S(1)}, bf16[64,1152]{1,0:T(8,128)(2,1)S(1)}, u32[]{:S(2)}, u32[]{:S(2)}) collective-permute-start(bf16[64,1152]{1,0:T(8,128)(2,1)S(1)} %get-tuple-element.57), channel_id=1, source_target_pairs={{0,8},{1,9},{2,10},{3,11},{4,12},{5,13},{6,14},{7,15},{8,16},{9,17... | collective-permute-start | bytes 442376 | tf_op jit(solution)/shard_map/ppermute | solution.py:24
  48.8 32.0 %collective-permute-start.9 = (bf16[64,1152]{1,0:T(8,128)(2,1)S(1)}, bf16[64,1152]{1,0:T(8,128)(2,1)S(1)}, u32[]{:S(2)}, u32[]{:S(2)}) collective-permute-start(bf16[64,1152]{1,0:T(8,128)(2,1)S(1)} %get-tuple-element.58), channel_id=1, source_target_pairs={{0,16},{1,17},{2,18},{3,19},{4,20},{5,21},{6,22},{7,23},{8,24},{9,... | collective-permute-start | bytes 442376 | tf_op jit(solution)/shard_map/ppermute | solution.py:24
  70.9 15.9 %collective-permute-start.12 = (bf16[64,512]{1,0:T(8,128)(2,1)S(1)}, bf16[64,512]{1,0:T(8,128)(2,1)S(1)}, u32[]{:S(2)}, u32[]{:S(2)}) collective-permute-start(bf16[64,512]{1,0:T(8,128)(2,1)S(1)} %get-tuple-element.66), channel_id=1, source_target_pairs={{2,0},{3,1},{4,2},{5,3},{6,4},{7,5},{8,6},{9,7},{10,8},{11,9},{12,... | collective-permute-start | bytes 196616 | tf_op jit(solution)/shard_map/ppermute | solution.py:24
  76.4 32.0 %collective-permute-start.13 = (bf16[64,512]{1,0:T(8,128)(2,1)S(1)}, bf16[64,512]{1,0:T(8,128)(2,1)S(1)}, u32[]{:S(2)}, u32[]{:S(2)}) collective-permute-start(bf16[64,512]{1,0:T(8,128)(2,1)S(1)} %get-tuple-element.67), channel_id=1, source_target_pairs={{2,0},{3,1},{4,2},{5,3},{6,4},{7,5},{8,6},{9,7},{10,8},{11,9},{12,... | collective-permute-start | bytes 196616 | tf_op jit(solution)/shard_map/ppermute | solution.py:24
  78.4 32.0 %collective-permute-start.14 = (bf16[64,512]{1,0:T(8,128)(2,1)S(1)}, bf16[64,512]{1,0:T(8,128)(2,1)S(1)}, u32[]{:S(2)}, u32[]{:S(2)}) collective-permute-start(bf16[64,512]{1,0:T(8,128)(2,1)S(1)} %get-tuple-element.68), channel_id=1, source_target_pairs={{4,0},{5,1},{6,2},{7,3},{8,4},{9,5},{10,6},{11,7},{12,8},{13,9},{1... | collective-permute-start | bytes 196616 | tf_op jit(solution)/shard_map/ppermute | solution.py:24
  80.8 31.4 %collective-permute-start.15 = (bf16[64,512]{1,0:T(8,128)(2,1)S(1)}, bf16[64,512]{1,0:T(8,128)(2,1)S(1)}, u32[]{:S(2)}, u32[]{:S(2)}) collective-permute-start(bf16[64,512]{1,0:T(8,128)(2,1)S(1)} %get-tuple-element.69), channel_id=1, source_target_pairs={{4,0},{5,1},{6,2},{7,3},{8,4},{9,5},{10,6},{11,7},{12,8},{13,9},{1... | collective-permute-start | bytes 196616 | tf_op jit(solution)/shard_map/ppermute | solution.py:24
  85.0 28.6 %collective-permute-start.16 = (bf16[64,512]{1,0:T(8,128)(2,1)S(1)}, bf16[64,512]{1,0:T(8,128)(2,1)S(1)}, u32[]{:S(2)}, u32[]{:S(2)}) collective-permute-start(bf16[64,512]{1,0:T(8,128)(2,1)S(1)} %get-tuple-element.70), channel_id=1, source_target_pairs={{8,0},{9,1},{10,2},{11,3},{12,4},{13,5},{14,6},{15,7},{16,8},{17,9... | collective-permute-start | bytes 196616 | tf_op jit(solution)/shard_map/ppermute | solution.py:24
  86.9 86.5 %collective-permute-start.10 = (bf16[320,512]{1,0:T(8,128)(2,1)S(1)}, bf16[320,512]{1,0:T(8,128)(2,1)S(1)}, u32[]{:S(2)}, u32[]{:S(2)}) collective-permute-start(bf16[320,512]{1,0:T(8,128)(2,1)S(1)} %get-tuple-element.64), channel_id=1, source_target_pairs={{1,0},{2,1},{3,2},{4,3},{5,4},{6,5},{7,6},{8,7},{9,8},{10,9},{11,1... | collective-permute-start | bytes 983048 | tf_op jit(solution)/shard_map/ppermute | solution.py:24
  108.4 66.3 %collective-permute-start.11 = (bf16[320,512]{1,0:T(8,128)(2,1)S(1)}, bf16[320,512]{1,0:T(8,128)(2,1)S(1)}, u32[]{:S(2)}, u32[]{:S(2)}) collective-permute-start(bf16[320,512]{1,0:T(8,128)(2,1)S(1)} %get-tuple-element.65), channel_id=1, source_target_pairs={{1,0},{2,1},{3,2},{4,3},{5,4},{6,5},{7,6},{8,7},{9,8},{10,9},{11,1... | collective-permute-start | bytes 983048 | tf_op jit(solution)/shard_map/ppermute | solution.py:24
  110.4 24.5 %collective-permute-start.17 = (bf16[64,512]{1,0:T(8,128)(2,1)S(1)}, bf16[64,512]{1,0:T(8,128)(2,1)S(1)}, u32[]{:S(2)}, u32[]{:S(2)}) collective-permute-start(bf16[64,512]{1,0:T(8,128)(2,1)S(1)} %get-tuple-element.71), channel_id=1, source_target_pairs={{8,0},{9,1},{10,2},{11,3},{12,4},{13,5},{14,6},{15,7},{16,8},{17,9... | collective-permute-start | bytes 196616 | tf_op jit(solution)/shard_map/ppermute | solution.py:24
  112.3 24.5 %collective-permute-start.18 = (bf16[64,512]{1,0:T(8,128)(2,1)S(1)}, bf16[64,512]{1,0:T(8,128)(2,1)S(1)}, u32[]{:S(2)}, u32[]{:S(2)}) collective-permute-start(bf16[64,512]{1,0:T(8,128)(2,1)S(1)} %get-tuple-element.72), channel_id=1, source_target_pairs={{16,0},{17,1},{18,2},{19,3},{20,4},{21,5},{22,6},{23,7},{24,8},{25... | collective-permute-start | bytes 196616 | tf_op jit(solution)/shard_map/ppermute | solution.py:24
  113.6 25.5 %collective-permute-start.19 = (bf16[64,512]{1,0:T(8,128)(2,1)S(1)}, bf16[64,512]{1,0:T(8,128)(2,1)S(1)}, u32[]{:S(2)}, u32[]{:S(2)}) collective-permute-start(bf16[64,512]{1,0:T(8,128)(2,1)S(1)} %get-tuple-element.73), channel_id=1, source_target_pairs={{16,0},{17,1},{18,2},{19,3},{20,4},{21,5},{22,6},{23,7},{24,8},{25... | collective-permute-start | bytes 196616 | tf_op jit(solution)/shard_map/ppermute | solution.py:24
  134.9 6.4 %collective-permute-start.22 = (bf16[64,512]{1,0:T(8,128)(2,1)S(1)}, bf16[64,512]{1,0:T(8,128)(2,1)S(1)}, u32[]{:S(2)}, u32[]{:S(2)}) collective-permute-start(bf16[64,512]{1,0:T(8,128)(2,1)S(1)} %get-tuple-element.79), channel_id=1, source_target_pairs={{2,0},{3,1},{4,2},{5,3},{6,4},{7,5},{8,6},{9,7},{10,8},{11,9},{12,... | collective-permute-start | bytes 196616 | tf_op jit(solution)/shard_map/ppermute | solution.py:24
  136.8 10.4 %collective-permute-start.23 = (bf16[64,512]{1,0:T(8,128)(2,1)S(1)}, bf16[64,512]{1,0:T(8,128)(2,1)S(1)}, u32[]{:S(2)}, u32[]{:S(2)}) collective-permute-start(bf16[64,512]{1,0:T(8,128)(2,1)S(1)} %get-tuple-element.80), channel_id=1, source_target_pairs={{2,0},{3,1},{4,2},{5,3},{6,4},{7,5},{8,6},{9,7},{10,8},{11,9},{12,... | collective-permute-start | bytes 196616 | tf_op jit(solution)/shard_map/ppermute | solution.py:24
  139.1 10.1 %collective-permute-start.24 = (bf16[64,512]{1,0:T(8,128)(2,1)S(1)}, bf16[64,512]{1,0:T(8,128)(2,1)S(1)}, u32[]{:S(2)}, u32[]{:S(2)}) collective-permute-start(bf16[64,512]{1,0:T(8,128)(2,1)S(1)} %get-tuple-element.81), channel_id=1, source_target_pairs={{4,0},{5,1},{6,2},{7,3},{8,4},{9,5},{10,6},{11,7},{12,8},{13,9},{1... | collective-permute-start | bytes 196616 | tf_op jit(solution)/shard_map/ppermute | solution.py:24
  141.3 38.9 %collective-permute-start.20 = (bf16[320,512]{1,0:T(8,128)(2,1)S(1)}, bf16[320,512]{1,0:T(8,128)(2,1)S(1)}, u32[]{:S(2)}, u32[]{:S(2)}) collective-permute-start(bf16[320,512]{1,0:T(8,128)(2,1)S(1)} %get-tuple-element.77), channel_id=1, source_target_pairs={{1,0},{2,1},{3,2},{4,3},{5,4},{6,5},{7,6},{8,7},{9,8},{10,9},{11,1... | collective-permute-start | bytes 983048 | tf_op jit(solution)/shard_map/ppermute | solution.py:24
  147.3 33.0 %collective-permute-start.21 = (bf16[320,512]{1,0:T(8,128)(2,1)S(1)}, bf16[320,512]{1,0:T(8,128)(2,1)S(1)}, u32[]{:S(2)}, u32[]{:S(2)}) collective-permute-start(bf16[320,512]{1,0:T(8,128)(2,1)S(1)} %get-tuple-element.78), channel_id=1, source_target_pairs={{1,0},{2,1},{3,2},{4,3},{5,4},{6,5},{7,6},{8,7},{9,8},{10,9},{11,1... | collective-permute-start | bytes 983048 | tf_op jit(solution)/shard_map/ppermute | solution.py:24
  149.2 16.7 %collective-permute-start.25 = (bf16[64,512]{1,0:T(8,128)(2,1)S(1)}, bf16[64,512]{1,0:T(8,128)(2,1)S(1)}, u32[]{:S(2)}, u32[]{:S(2)}) collective-permute-start(bf16[64,512]{1,0:T(8,128)(2,1)S(1)} %get-tuple-element.82), channel_id=1, source_target_pairs={{4,0},{5,1},{6,2},{7,3},{8,4},{9,5},{10,6},{11,7},{12,8},{13,9},{1... | collective-permute-start | bytes 196616 | tf_op jit(solution)/shard_map/ppermute | solution.py:24
  165.9 3.8 %collective-permute-start.26 = (bf16[64,512]{1,0:T(8,128)(2,1)S(1)}, bf16[64,512]{1,0:T(8,128)(2,1)S(1)}, u32[]{:S(2)}, u32[]{:S(2)}) collective-permute-start(bf16[64,512]{1,0:T(8,128)(2,1)S(1)} %get-tuple-element.83), channel_id=1, source_target_pairs={{8,0},{9,1},{10,2},{11,3},{12,4},{13,5},{14,6},{15,7},{16,8},{17,9... | collective-permute-start | bytes 196616 | tf_op jit(solution)/shard_map/ppermute | solution.py:24
  169.7 10.5 %collective-permute-start.27 = (bf16[64,512]{1,0:T(8,128)(2,1)S(1)}, bf16[64,512]{1,0:T(8,128)(2,1)S(1)}, u32[]{:S(2)}, u32[]{:S(2)}) collective-permute-start(bf16[64,512]{1,0:T(8,128)(2,1)S(1)} %get-tuple-element.84), channel_id=1, source_target_pairs={{8,0},{9,1},{10,2},{11,3},{12,4},{13,5},{14,6},{15,7},{16,8},{17,9... | collective-permute-start | bytes 196616 | tf_op jit(solution)/shard_map/ppermute | solution.py:24
  173.4 6.8 %collective-permute-start.28 = (bf16[64,512]{1,0:T(8,128)(2,1)S(1)}, bf16[64,512]{1,0:T(8,128)(2,1)S(1)}, u32[]{:S(2)}, u32[]{:S(2)}) collective-permute-start(bf16[64,512]{1,0:T(8,128)(2,1)S(1)} %get-tuple-element.85), channel_id=1, source_target_pairs={{16,0},{17,1},{18,2},{19,3},{20,4},{21,5},{22,6},{23,7},{24,8},{25... | collective-permute-start | bytes 196616 | tf_op jit(solution)/shard_map/ppermute | solution.py:24
  174.7 5.5 %collective-permute-start.29 = (bf16[64,512]{1,0:T(8,128)(2,1)S(1)}, bf16[64,512]{1,0:T(8,128)(2,1)S(1)}, u32[]{:S(2)}, u32[]{:S(2)}) collective-permute-start(bf16[64,512]{1,0:T(8,128)(2,1)S(1)} %get-tuple-element.86), channel_id=1, source_target_pairs={{16,0},{17,1},{18,2},{19,3},{20,4},{21,5},{22,6},{23,7},{24,8},{25... | collective-permute-start | bytes 196616 | tf_op jit(solution)/shard_map/ppermute | solution.py:24
  176.0 1.6 copy-start.3
  (5 other events, 4.1 us)

commit v2 on v1

v2 whole, which is shorter than its diff:
```python
import functools

import jax
import jax.numpy as jnp
from jax import lax
from jax.experimental import pallas as pl
from jax.experimental.pallas import tpu as pltpu
from jax.sharding import PartitionSpec as P

WIN = 256
BLK = 64
ROWS = 128
LANES = 128
DEAD = -1e30
AHEAD = 3
AXES = ("grp", "seq")
F32 = jnp.float32
BF16 = jnp.bfloat16


def nt(a, b):
    return lax.dot_general(a, b, (((1,), (1,)), ((), ())), preferred_element_type=F32)


def nn(a, b):
    return lax.dot_general(a, b, (((1,), (0,)), ((), ())), preferred_element_type=F32)


def block_rows_of(start, rows):
    t = lax.broadcasted_iota(jnp.int32, (BLK, rows), 0)
    j = lax.broadcasted_iota(jnp.int32, (BLK, rows), 1)
    return (j - t == start).astype(F32).astype(BF16)


def merged(pair):
    half = LANES // 2
    return jnp.concatenate([pair[:half, :ROWS], pair[half:, ROWS:]], axis=0)


def attend_pair(head, scale, q, do, near_k, near_v, far_k, far_v, near_kt, near_vt, far_kt, far_vt,
                dot, out, dq, near_dk, near_dv, far_dk, far_dv):
    rows = q.shape[0]
    half = LANES // 2
    lane = lax.broadcasted_iota(jnp.int32, (ROWS, LANES), 1)
    first = lane < half
    ones = jnp.concatenate([(lane == head).astype(F32), (lane == head + 1).astype(F32)], axis=0)
    ones = ones.astype(BF16)
    span_row = lax.broadcasted_iota(jnp.int32, (ROWS, 2 * ROWS), 0)
    query_col = lax.broadcasted_iota(jnp.int32, (ROWS, 2 * ROWS), 1) & (ROWS - 1)
    below, above = span_row >= query_col, span_row <= query_col
    span = WIN + ROWS
    zero = jnp.zeros((ROWS, LANES), BF16)
    near_dk[...] = jnp.zeros_like(near_dk)
    near_dv[...] = jnp.zeros_like(near_dv)
    for b in range(rows // ROWS):
        mine = slice(b * ROWS, (b + 1) * ROWS)
        seen = slice(b * ROWS, b * ROWS + span)
        qb = (q[mine, :].astype(F32) * scale).astype(BF16)
        db = do[mine, :]
        q2 = jnp.concatenate([jnp.where(first, qb, zero), jnp.where(first, zero, qb)], axis=0)
        d2 = jnp.concatenate([jnp.where(first, db, zero), jnp.where(first, zero, db)], axis=0)
        qc = jnp.concatenate([q2, ones], axis=1)
        sn = nt(near_k[seen, :], qc)
        sf = nt(far_k[...], qc)
        sn = jnp.concatenate(
            [
                jnp.where(below, sn[:ROWS], DEAD),
                sn[ROWS:WIN],
                jnp.where(above, sn[WIN:], DEAD),
            ],
            axis=0,
        )
        top = jnp.maximum(jnp.max(sn, axis=0, keepdims=True), jnp.max(sf, axis=0, keepdims=True))
        en = jnp.exp(sn - top)
        ef = jnp.exp(sf - top)
        total = jnp.sum(en, axis=0, keepdims=True) + jnp.sum(ef, axis=0, keepdims=True)
        share = 1.0 / total
        wn, wf = en * share, ef * share
        rn, rf = wn.astype(BF16), wf.astype(BF16)
        att = merged(nn(near_vt[:, seen], rn) + nn(far_vt[...], rf))
        out[mine, :] = att.T.astype(out.dtype)
        parts = att * dot[:, mine]
        row_dot = jnp.concatenate(
            [
                jnp.sum(parts[:half], axis=0, keepdims=True),
                jnp.sum(parts[half:], axis=0, keepdims=True),
            ],
            axis=1,
        )
        gn = (wn * (nt(near_v[seen, :], d2) - row_dot)).astype(BF16)
        gf = (wf * (nt(far_v[...], d2) - row_dot)).astype(BF16)
        dqt = merged(nn(near_kt[:, seen], gn) + nn(far_kt[...], gf)) * scale
        dq[mine, :] = dqt.T.astype(dq.dtype)
        near_dk[seen, :] += nn(gn, q2)
        near_dv[seen, :] += nn(rn, d2)
        if b == 0:
            far_dk[...] = nn(gf, q2)
            far_dv[...] = nn(rf, d2)
        else:
            far_dk[...] += nn(gf, q2)
            far_dv[...] += nn(rf, d2)


def tn(a, b):
    return lax.dot_general(a, b, (((0,), (0,)), ((), ())), preferred_element_type=F32)


def kernel(levels, scale, starts, ids, table, q, k, v, do, out, dq, dk, dv, bias, padded,
           send_f, recv_f, send_bias, recv_bias, send_b, recv_b, own,
           near_k, near_v, far_k, far_v, near_kt, near_vt, far_kt, far_vt, dot,
           near_dk, near_dv, far_dk, far_dv,
           sem_fs, sem_fr, sem_bias_s, sem_bias_r, sem_bs, sem_br):
    rows, width_all = q.shape
    pairs = width_all // LANES
    ahead = min(AHEAD, pairs)
    types, heads = table.shape
    lines = lax.axis_size("seq")
    count = lax.axis_size("grp") * lines
    position = lax.axis_index("grp") * lines + lax.axis_index("seq")
    depth = [BLK + (WIN if e == 0 else 0) for e in range(levels)]
    offset = [sum(depth[:e]) for e in range(levels)]
    spot = [pl.ds(offset[e], depth[e]) for e in range(levels)]

    def device(index):
        return (lax.div(index, lines), lax.rem(index, lines))

    def takes(e):
        return position >= 2**e

    def gives(e):
        return position + 2**e < count

    def copy(src, dst, send, recv, index):
        return pltpu.make_async_remote_copy(
            src_ref=src, dst_ref=dst, send_sem=send, recv_sem=recv,
            device_id=device(index), device_id_type=pl.DeviceIdType.MESH,
        )

    def ahead_copy(p, e):
        return copy(send_f.at[p, spot[e]], recv_f.at[p, spot[e]], sem_fs.at[p, e],
                    sem_fr.at[p, e], position + 2**e)

    def bias_copy(e):
        return copy(send_bias.at[spot[e]], recv_bias.at[spot[e]], sem_bias_s.at[e],
                    sem_bias_r.at[e], position + 2**e)

    def back_copy(p, e):
        return copy(send_b.at[p, spot[e]], recv_b.at[p, spot[e]], sem_bs.at[p, e],
                    sem_br.at[p, e], position - 2**e)

    barrier = pltpu.get_barrier_semaphore()
    for e in range(levels):

        @pl.when(gives(e))
        def _():
            pl.semaphore_signal(barrier, inc=1, device_id=device(position + 2**e),
                                device_id_type=pl.DeviceIdType.MESH)

        @pl.when(takes(e))
        def _():
            pl.semaphore_signal(barrier, inc=1, device_id=device(position - 2**e),
                                device_id_type=pl.DeviceIdType.MESH)

    padded[...] = jnp.zeros_like(padded)
    padded[:, :heads] = table[...].astype(BF16).astype(F32)
    kind = lax.broadcasted_iota(jnp.int32, (types, rows), 0)
    onehot = (kind == ids[...]).astype(F32).astype(BF16)
    bias[...] = tn(onehot, padded[...].astype(BF16)).astype(BF16)
    for e in range(levels):
        pick = block_rows_of(starts[0, e], rows)
        send_bias[offset[e] : offset[e] + BLK, :] = nn(pick, bias[...]).astype(BF16)
        if e == 0:
            send_bias[BLK : BLK + WIN, :] = bias[rows - WIN :, :]

        @pl.when(jnp.logical_not(takes(e)))
        def _():
            recv_bias[spot[e], :] = jnp.full((depth[e], LANES), DEAD, BF16)

            def clear(p, carry):
                recv_f[p, spot[e], :] = jnp.zeros((depth[e], 2 * LANES), BF16)
                return carry

            lax.fori_loop(0, pairs, clear, 0)

        @pl.when(jnp.logical_not(gives(e)))
        def _():
            def clear(p, carry):
                recv_b[p, spot[e], :] = jnp.zeros((depth[e], 2 * LANES), BF16)
                return carry

            lax.fori_loop(0, pairs, clear, 0)

    def columns(p):
        return pl.ds(pl.multiple_of(p * LANES, LANES), LANES)

    def gather(p):
        both = jnp.concatenate([k[:, columns(p)], v[:, columns(p)]], axis=1)
        for e in range(levels):
            pick = block_rows_of(starts[0, e], rows)
            send_f[p, offset[e] : offset[e] + BLK, :] = nn(pick, both).astype(BF16)
            if e == 0:
                send_f[p, BLK : BLK + WIN, :] = both[rows - WIN :]

    def send_ahead(p):
        for e in range(levels):

            @pl.when(gives(e))
            def _():
                ahead_copy(p, e).start()

    gather(0)
    greeted = 0
    for e in range(levels):
        greeted = greeted + gives(e).astype(jnp.int32) + takes(e).astype(jnp.int32)
    pl.semaphore_wait(barrier, greeted)
    for e in range(levels):

        @pl.when(gives(e))
        def _():
            bias_copy(e).start()

    send_ahead(0)

    def early(p, carry):
        gather(p)
        send_ahead(p)
        return carry

    lax.fori_loop(1, ahead, early, 0)
    for e in range(levels):

        @pl.when(takes(e))
        def _():
            bias_copy(e).wait_recv()

    near_k[:WIN, LANES:] = recv_bias[BLK : BLK + WIN, :]
    near_k[WIN:, LANES:] = bias[...]
    for e in range(levels):
        far_k[e * BLK : (e + 1) * BLK, LANES:] = recv_bias[offset[e] : offset[e] + BLK, :]

    def one_pair(p, carry):
        @pl.when(p + ahead < pairs)
        def _():
            gather(p + ahead)
            send_ahead(p + ahead)

        mine = columns(p)
        near_k[WIN:, :LANES] = k[:, mine]
        near_v[WIN:, :] = v[:, mine]
        dot[...] = do[:, mine].astype(F32).T
        for e in range(levels):

            @pl.when(takes(e))
            def _():
                ahead_copy(p, e).wait_recv()

        for e in range(levels):
            at = slice(e * BLK, (e + 1) * BLK)
            far_k[at, :LANES] = recv_f[p, offset[e] : offset[e] + BLK, :LANES]
            far_v[at, :] = recv_f[p, offset[e] : offset[e] + BLK, LANES:]
        near_k[:WIN, :LANES] = recv_f[p, BLK : BLK + WIN, :LANES]
        near_v[:WIN, :] = recv_f[p, BLK : BLK + WIN, LANES:]
        near_kt[...] = near_k[:, :LANES].T
        near_vt[...] = near_v[...].T
        far_kt[...] = far_k[:, :LANES].T
        far_vt[...] = far_v[...].T
        attend_pair(2 * p, scale, q.at[:, mine], do.at[:, mine], near_k, near_v, far_k, far_v,
                    near_kt, near_vt, far_kt, far_vt, dot, out.at[:, mine], dq.at[:, mine],
                    near_dk, near_dv, far_dk, far_dv)
        for e in range(levels):
            at = slice(e * BLK, (e + 1) * BLK)
            send_b[p, offset[e] : offset[e] + BLK, :LANES] = far_dk[at, :].astype(BF16)
            send_b[p, offset[e] : offset[e] + BLK, LANES:] = far_dv[at, :].astype(BF16)
            if e == 0:
                send_b[p, BLK : BLK + WIN, :LANES] = near_dk[:WIN, :].astype(BF16)
                send_b[p, BLK : BLK + WIN, LANES:] = near_dv[:WIN, :].astype(BF16)

            @pl.when(takes(e))
            def _():
                back_copy(p, e).start()

        own[p, :, :LANES] = near_dk[WIN:, :]
        own[p, :, LANES:] = near_dv[WIN:, :]
        return carry

    lax.fori_loop(0, pairs, one_pair, 0)

    def settle(p, carry):
        for e in range(levels):

            @pl.when(gives(e))
            def _():
                back_copy(p, e).wait_recv()

        total = own[p]
        for e in range(levels):
            total = total + tn(
                block_rows_of(starts[0, e], rows), recv_b[p, offset[e] : offset[e] + BLK, :]
            )
        first = rows - WIN
        last = total[first:] + recv_b[p, BLK : BLK + WIN, :].astype(F32)
        mine = columns(p)
        dk[:first, mine] = total[:first, :LANES].astype(BF16)
        dv[:first, mine] = total[:first, LANES:].astype(BF16)
        dk[first:, mine] = last[:, :LANES].astype(BF16)
        dv[first:, mine] = last[:, LANES:].astype(BF16)
        return carry

    lax.fori_loop(0, pairs, settle, 0)

    def sent(p, carry):
        for e in range(levels):

            @pl.when(gives(e))
            def _():
                ahead_copy(p, e).wait_send()

            @pl.when(takes(e))
            def _():
                back_copy(p, e).wait_send()

        return carry

    lax.fori_loop(0, pairs, sent, 0)
    for e in range(levels):

        @pl.when(gives(e))
        def _():
            bias_copy(e).wait_send()


def local(queries, keys, values, event_ids, type_bias, block_start, d_out):
    rows, width_all = queries.shape
    types, heads = type_bias.shape
    levels = block_start.shape[1]
    scale = (width_all // heads) ** -0.5
    pairs = width_all // LANES
    far = levels * BLK
    sent = far + WIN
    smem = pl.BlockSpec(memory_space=pltpu.SMEM)
    vmem = pl.BlockSpec(memory_space=pltpu.VMEM)
    dma = pltpu.SemaphoreType.DMA
    return pl.pallas_call(
        functools.partial(kernel, levels, scale),
        out_shape=[jax.ShapeDtypeStruct((rows, width_all), BF16)] * 4,
        in_specs=[smem] + [vmem] * 6,
        out_specs=[vmem] * 4,
        scratch_shapes=[
            pltpu.VMEM((rows, LANES), BF16),
            pltpu.VMEM((types, LANES), F32),
            pltpu.VMEM((pairs, sent, 2 * LANES), BF16),
            pltpu.VMEM((pairs, sent, 2 * LANES), BF16),
            pltpu.VMEM((sent, LANES), BF16),
            pltpu.VMEM((sent, LANES), BF16),
            pltpu.VMEM((pairs, sent, 2 * LANES), BF16),
            pltpu.VMEM((pairs, sent, 2 * LANES), BF16),
            pltpu.VMEM((pairs, rows, 2 * LANES), F32),
            pltpu.VMEM((WIN + rows, 2 * LANES), BF16),
            pltpu.VMEM((WIN + rows, LANES), BF16),
            pltpu.VMEM((far, 2 * LANES), BF16),
            pltpu.VMEM((far, LANES), BF16),
            pltpu.VMEM((LANES, WIN + rows), BF16),
            pltpu.VMEM((LANES, WIN + rows), BF16),
            pltpu.VMEM((LANES, far), BF16),
            pltpu.VMEM((LANES, far), BF16),
            pltpu.VMEM((LANES, rows), F32),
            pltpu.VMEM((WIN + rows, LANES), F32),
            pltpu.VMEM((WIN + rows, LANES), F32),
            pltpu.VMEM((far, LANES), F32),
            pltpu.VMEM((far, LANES), F32),
            dma((pairs, levels)),
            dma((pairs, levels)),
            dma((levels,)),
            dma((levels,)),
            dma((pairs, levels)),
            dma((pairs, levels)),
        ],
        compiler_params=pltpu.CompilerParams(
            vmem_limit_bytes=56 * 2**20, collective_id=0, has_side_effects=True
        ),
        cost_estimate=pl.CostEstimate(
            flops=12 * rows * (WIN + ROWS + far) * width_all,
            bytes_accessed=16 * rows * width_all,
            transcendentals=rows * (WIN + ROWS + far) * heads,
        ),
        name="attend",
    )(block_start, event_ids[None, :], type_bias, queries, keys, values, d_out)


def solution(mesh):
    rows = P(AXES, None)
    return jax.shard_map(
        local,
        mesh=mesh,
        in_specs=(rows, rows, rows, P(AXES), P(), rows, rows),
        out_specs=(rows, rows, rows, rows),
        check_vma=False,
    )
```

time: 187 us -> 103 us (0.55); the launches traced: 184 us -> 103 us
  starting transfers between devices: 108 us -> 0 us
  Pallas kernels: 48.5 us -> 94.4 us
  waiting for transfers between devices: 17 us -> 0 us
  other arithmetic: 3.16 us -> 0 us
  local copies, waits for them, and re-layouts: 6.21 us -> 8.12 us
    ppermute x30 -> x0, starting transfers between devices: 108 us -> none  [passed_along(): lax.ppermute(value, axis, [(source, source + steps) for source in range(i...]
    pallas_call x5 -> x1, Pallas kernels: 48.5 us -> 94.4 us  [local(): pl.pallas_call(functools.partial(kernel, levels, scale), out_shape=[jax.S...]
    ppermute x30 -> x0, waiting for transfers between devices: 17 us -> none  [passed_along(): lax.ppermute(value, axis, [(source, source + steps) for source in range(i...]
    concatenate x2 -> x0, other arithmetic: 3.16 us -> none  [local(): jnp.concatenate(list(chunk), axis=1)]
    unnamed x15 -> x11, local copies, waits for them, and re-layouts: 6.21 us -> 8.12 us
  transfers between devices with their start and end apart: 30 -> 0, of which waited for: 3 -> 0; matrix products, arithmetic and copies ran while one was open for 1% -> 0% of each run, Pallas kernels for 23% -> 0%
where the time goes in v2:
time: 103 us
  Pallas kernels  94.4 us (92%)
  local copies, waits for them, and re-layouts  8.12 us (8%)
    pallas_call x1, Pallas kernels, local(): pl.pallas_call(functools.partial(kernel, levels, scale), out_shape=[jax.S...  94.4 us
    unnamed x11, local copies, waits for them, and re-layouts  8.12 us

profile of v2, /device:TPU:2, one launch (start us, length us, event | category | flops | bytes accessed | tf_op | source)
XLA Modules:
  0.0 103.2 jit_solution(11153766171574694272)
XLA Ops:
  0.6 1.6 %copy.11.table = f32[512,16]{1,0:T(8,128)} copy(f32[512,16]{0,1:T(8,128)} %param.11) | data formatting | bytes 65536 | tf_op args[4]
  2.2 94.4 %attend.1 = (bf16[512,1024]{1,0:T(8,128)(2,1)}, bf16[512,1024]{1,0:T(8,128)(2,1)}, bf16[512,1024]{1,0:T(8,128)(2,1)}, bf16[512,1024]{1,0:T(8,128)(2,1)}) custom-call(s32[1,5]{1,0:T(1,128)} %starts.1, s32[1,512]{1,0:T(1,128)} %bitcast.1, f32[512,16]{1,0:T(8,128)} %copy.11.table, bf16[512,1024]{1,0:T(8,128)(2,1)} %q.1, bf16[512,1024]{1,0:T(8,128)(2,1)} %k.1, ...), custom_call_target="tpu_custom_call" | custom-call | flops 4429185024 | bytes 8388608 | tf_op jit(solution)/shard_map/attend/pallas_call | solution.py:343
  96.6 0.0 copy-start.2
  96.6 2.4 %copy.16 = bf16[512,1024]{1,0:T(8,128)(2,1)} copy(bf16[512,1024]{1,0:T(8,128)(2,1)} %get-tuple-element.8) | data formatting | bytes 2097152
  99.0 0.0 copy-done.2
  99.0 0.0 copy-start.1
  99.0 1.0 copy.17
  100.0 0.6 copy-done.1
  100.6 0.0 copy-start
  100.6 1.0 copy.18
  101.6 0.6 copy-done
  102.2 1.0 copy.19
Async XLA Ops:
  96.6 2.4 %copy-start.2 = (bf16[512,1024]{1,0:T(8,128)(2,1)S(1)}, bf16[512,1024]{1,0:T(8,128)(2,1)}, u32[]{:S(2)}) copy-start(bf16[512,1024]{1,0:T(8,128)(2,1)} %get-tuple-element.9) | copy-start | bytes 3145732
  99.0 1.6 %copy-start.1 = (bf16[512,1024]{1,0:T(8,128)(2,1)S(1)}, bf16[512,1024]{1,0:T(8,128)(2,1)}, u32[]{:S(2)}) copy-start(bf16[512,1024]{1,0:T(8,128)(2,1)} %get-tuple-element.10) | copy-start | bytes 3145732
  100.6 1.6 %copy-start = (bf16[512,1024]{1,0:T(8,128)(2,1)S(1)}, bf16[512,1024]{1,0:T(8,128)(2,1)}, u32[]{:S(2)}) copy-start(bf16[512,1024]{1,0:T(8,128)(2,1)} %get-tuple-element.11) | copy-start | bytes 3145732

commit v3 on v2

--- a/solution.py
+++ b/solution.py
@@ -12,7 +12,7 @@
 ROWS = 128
 LANES = 128
 DEAD = -1e30
-AHEAD = 3
+AHEAD = 1
 AXES = ("grp", "seq")
 F32 = jnp.float32
 BF16 = jnp.bfloat16
@@ -161,6 +161,30 @@
             pl.semaphore_signal(barrier, inc=1, device_id=device(position - 2**e),
                                 device_id_type=pl.DeviceIdType.MESH)
 
+    def columns(p):
+        return pl.ds(pl.multiple_of(p * LANES, LANES), LANES)
+
+    def gather(p):
+        both = jnp.concatenate([k[:, columns(p)], v[:, columns(p)]], axis=1)
+        for e in range(levels):
+            pick = block_rows_of(starts[0, e], rows)
+            send_f[p, offset[e] : offset[e] + BLK, :] = nn(pick, both).astype(BF16)
+            if e == 0:
+                send_f[p, BLK : BLK + WIN, :] = both[rows - WIN :]
+
+    def send_ahead(p):
+        for e in range(levels):
+
+            @pl.when(gives(e))
+            def _():
+                ahead_copy(p, e).start()
+
+    gather(0)
+    greeted = 0
+    for e in range(levels):
+        greeted = greeted + gives(e).astype(jnp.int32) + takes(e).astype(jnp.int32)
+    pl.semaphore_wait(barrier, greeted)
+    send_ahead(0)
     padded[...] = jnp.zeros_like(padded)
     padded[:, :heads] = table[...].astype(BF16).astype(F32)
     kind = lax.broadcasted_iota(jnp.int32, (types, rows), 0)
@@ -190,36 +214,11 @@
 
             lax.fori_loop(0, pairs, clear, 0)
 
-    def columns(p):
-        return pl.ds(pl.multiple_of(p * LANES, LANES), LANES)
-
-    def gather(p):
-        both = jnp.concatenate([k[:, columns(p)], v[:, columns(p)]], axis=1)
-        for e in range(levels):
-            pick = block_rows_of(starts[0, e], rows)
-            send_f[p, offset[e] : offset[e] + BLK, :] = nn(pick, both).astype(BF16)
-            if e == 0:
-                send_f[p, BLK : BLK + WIN, :] = both[rows - WIN :]
-
-    def send_ahead(p):
-        for e in range(levels):
-
-            @pl.when(gives(e))
-            def _():
-                ahead_copy(p, e).start()
-
-    gather(0)
-    greeted = 0
-    for e in range(levels):
-        greeted = greeted + gives(e).astype(jnp.int32) + takes(e).astype(jnp.int32)
-    pl.semaphore_wait(barrier, greeted)
     for e in range(levels):
 
         @pl.when(gives(e))
         def _():
             bias_copy(e).start()
-
-    send_ahead(0)
 
     def early(p, carry):
         gather(p)
@@ -239,11 +238,6 @@
         far_k[e * BLK : (e + 1) * BLK, LANES:] = recv_bias[offset[e] : offset[e] + BLK, :]
 
     def one_pair(p, carry):
-        @pl.when(p + ahead < pairs)
-        def _():
-            gather(p + ahead)
-            send_ahead(p + ahead)
-
         mine = columns(p)
         near_k[WIN:, :LANES] = k[:, mine]
         near_v[WIN:, :] = v[:, mine]
@@ -253,6 +247,11 @@
             @pl.when(takes(e))
             def _():
                 ahead_copy(p, e).wait_recv()
+
+        @pl.when(p + ahead < pairs)
+        def _():
+            gather(p + ahead)
+            send_ahead(p + ahead)
 
         for e in range(levels):
             at = slice(e * BLK, (e + 1) * BLK)
@@ -329,6 +328,11 @@
             bias_copy(e).wait_send()
 
 
+def hand_over(*refs):
+    for source, target in zip(refs[:4], refs[4:]):
+        target[...] = source[...]
+
+
 def local(queries, keys, values, event_ids, type_bias, block_start, d_out):
     rows, width_all = queries.shape
     types, heads = type_bias.shape
@@ -340,7 +344,7 @@
     smem = pl.BlockSpec(memory_space=pltpu.SMEM)
     vmem = pl.BlockSpec(memory_space=pltpu.VMEM)
     dma = pltpu.SemaphoreType.DMA
-    return pl.pallas_call(
+    held = pl.pallas_call(
         functools.partial(kernel, levels, scale),
         out_shape=[jax.ShapeDtypeStruct((rows, width_all), BF16)] * 4,
         in_specs=[smem] + [vmem] * 6,
@@ -385,6 +389,15 @@
         ),
         name="attend",
     )(block_start, event_ids[None, :], type_bias, queries, keys, values, d_out)
+    part = pl.BlockSpec((ROWS, width_all), lambda i: (i, 0))
+    return pl.pallas_call(
+        hand_over,
+        grid=(rows // ROWS,),
+        out_shape=[jax.ShapeDtypeStruct((rows, width_all), BF16)] * 4,
+        in_specs=[part] * 4,
+        out_specs=[part] * 4,
+        name="hand_over",
+    )(*held)
 
 
 def solution(mesh):

time: 103 us -> 94.7 us (0.919)
  local copies, waits for them, and re-layouts: 8.12 us -> 1.59 us
  Pallas kernels: 94.4 us -> 92.2 us
    pallas_call x1, Pallas kernels: 94.4 us -> 87.5 us  [local(): pl.pallas_call(functools.partial(kernel, levels, scale), out_shape=[jax.S...]
    unnamed x11 -> x1, local copies, waits for them, and re-layouts: 8.12 us -> 1.59 us
    pallas_call x0 -> x1, Pallas kernels: none -> 4.66 us  [local(): pl.pallas_call(hand_over, grid=(rows // ROWS,), out_shape=[jax.ShapeDtype...]
where the time goes in v3:
time: 94.7 us; the launch traced here: 94.4 us
  Pallas kernels  92.2 us (97%)
  local copies, waits for them, and re-layouts  1.59 us (2%)
    pallas_call x1, Pallas kernels, local(): pl.pallas_call(functools.partial(kernel, levels, scale), out_shape=[jax.S...  87.5 us
    pallas_call x1, Pallas kernels, local(): pl.pallas_call(hand_over, grid=(rows // ROWS,), out_shape=[jax.ShapeDtype...  4.66 us

profile of v3, /device:TPU:2, one launch (start us, length us, event | category | flops | bytes accessed | tf_op | source)
XLA Modules:
  0.0 94.4 jit_solution(13911005707758557928)
XLA Ops:
  0.6 1.6 %copy.11.table = f32[512,16]{1,0:T(8,128)} copy(f32[512,16]{0,1:T(8,128)} %param.11) | data formatting | bytes 65536 | tf_op args[4]
  2.2 87.5 %attend.1 = (bf16[512,1024]{1,0:T(8,128)(2,1)}, bf16[512,1024]{1,0:T(8,128)(2,1)}, bf16[512,1024]{1,0:T(8,128)(2,1)}, bf16[512,1024]{1,0:T(8,128)(2,1)}) custom-call(s32[1,5]{1,0:T(1,128)} %starts.1, s32[1,512]{1,0:T(1,128)} %bitcast.1, f32[512,16]{1,0:T(8,128)} %copy.11.table, bf16[512,1024]{1,0:T(8,128)(2,1)} %q.1, bf16[512,1024]{1,0:T(8,128)(2,1)} %k.1, ...), custom_call_target="tpu_custom_call" | custom-call | flops 4429185024 | bytes 8388608 | tf_op jit(solution)/shard_map/attend/pallas_call | solution.py:347
  89.7 4.7 %hand_over.1 = (bf16[512,1024]{1,0:T(8,128)(2,1)}, bf16[512,1024]{1,0:T(8,128)(2,1)}, bf16[512,1024]{1,0:T(8,128)(2,1)}, bf16[512,1024]{1,0:T(8,128)(2,1)}) custom-call(bf16[512,1024]{1,0:T(8,128)(2,1)} %get-tuple-element.8.refs_0_, bf16[512,1024]{1,0:T(8,128)(2,1)} %get-tuple-element.9.refs_1_, bf16[512,1024]{1,0:T(8,128)(2,1)} %get-tuple-element.10.refs_2_, ...), custom_call_target="tpu_custom_call" | custom-call | tf_op jit(solution)/shard_map/hand_over/pallas_call | solution.py:393

commit v4 on v3

--- a/solution.py
+++ b/solution.py
@@ -238,6 +238,10 @@
         far_k[e * BLK : (e + 1) * BLK, LANES:] = recv_bias[offset[e] : offset[e] + BLK, :]
 
     def one_pair(p, carry):
+        @pl.when(p + ahead < pairs)
+        def _():
+            gather(p + ahead)
+
         mine = columns(p)
         near_k[WIN:, :LANES] = k[:, mine]
         near_v[WIN:, :] = v[:, mine]
@@ -250,7 +254,6 @@
 
         @pl.when(p + ahead < pairs)
         def _():
-            gather(p + ahead)
             send_ahead(p + ahead)
 
         for e in range(levels):

time: 94.7 us -> 93.5 us (0.987)
  Pallas kernels: 92.2 us -> 90.7 us
    pallas_call x1, Pallas kernels: 87.5 us -> 86 us  [local(): pl.pallas_call(functools.partial(kernel, levels, scale), out_shape=[jax.S...]
where the time goes in v4:
time: 93.5 us; the launch traced here: 92.9 us
  Pallas kernels  90.7 us (97%)
  local copies, waits for them, and re-layouts  1.59 us (2%)
    pallas_call x1, Pallas kernels, local(): pl.pallas_call(functools.partial(kernel, levels, scale), out_shape=[jax.S...  86 us
    pallas_call x1, Pallas kernels, local(): pl.pallas_call(hand_over, grid=(rows // ROWS,), out_shape=[jax.ShapeDtype...  4.66 us

profile of v4, /device:TPU:2, one launch (start us, length us, event | category | flops | bytes accessed | tf_op | source)
XLA Modules:
  0.0 92.9 jit_solution(4386102622232574376)
XLA Ops:
  0.6 1.6 %copy.11.table = f32[512,16]{1,0:T(8,128)} copy(f32[512,16]{0,1:T(8,128)} %param.11) | data formatting | bytes 65536 | tf_op args[4]
  2.2 86.0 %attend.1 = (bf16[512,1024]{1,0:T(8,128)(2,1)}, bf16[512,1024]{1,0:T(8,128)(2,1)}, bf16[512,1024]{1,0:T(8,128)(2,1)}, bf16[512,1024]{1,0:T(8,128)(2,1)}) custom-call(s32[1,5]{1,0:T(1,128)} %starts.1, s32[1,512]{1,0:T(1,128)} %bitcast.1, f32[512,16]{1,0:T(8,128)} %copy.11.table, bf16[512,1024]{1,0:T(8,128)(2,1)} %q.1, bf16[512,1024]{1,0:T(8,128)(2,1)} %k.1, ...), custom_call_target="tpu_custom_call" | custom-call | flops 4429185024 | bytes 8388608 | tf_op jit(solution)/shard_map/attend/pallas_call | solution.py:350
  88.2 4.7 %hand_over.1 = (bf16[512,1024]{1,0:T(8,128)(2,1)}, bf16[512,1024]{1,0:T(8,128)(2,1)}, bf16[512,1024]{1,0:T(8,128)(2,1)}, bf16[512,1024]{1,0:T(8,128)(2,1)}) custom-call(bf16[512,1024]{1,0:T(8,128)(2,1)} %get-tuple-element.8.refs_0_, bf16[512,1024]{1,0:T(8,128)(2,1)} %get-tuple-element.9.refs_1_, bf16[512,1024]{1,0:T(8,128)(2,1)} %get-tuple-element.10.refs_2_, ...), custom_call_target="tpu_custom_call" | custom-call | tf_op jit(solution)/shard_map/hand_over/pallas_call | solution.py:396
